TPU v7x, 256 devices: a whole 4x4x8 slice. The times are simulated.
256 devices in a mesh: inline: 32 (over x, z), xline: 8 (over y, core).
Axes of the slice: x: 4, y: 4, z: 8, core: 2. Of those that a mesh axis runs over, the one named last changes fastest.
Arguments:
- traces: bfloat16 [131072, 1024], P(('inline', 'xline')), may hold values from -6 to 6
- destination: int32 [131072, 1], P(('inline', 'xline')), may hold values from 0 to 255; in each aligned block of 512 rows (0 to 511, 512 to 1023, ...) at most 6 rows name the same one
- bin_local: int32 [131072], P(('inline', 'xline')), may hold values from 0 to 63
- offset_class: int32 [131072], P(('inline', 'xline')), may hold values from 0 to 7
- dip_inline: int32 [128, 128], P('inline', 'xline'), may hold values from -3 to 3
- dip_xline: int32 [128, 128], P('inline', 'xline'), may hold values from -3 to 3
Outputs:
- smoothed: float32 [8, 128, 128, 1024], P(None, 'inline', 'xline')
Inputs may be any that keep to these rules, and one draw needn't show every extreme that they name: Among the traces of one device no destination occurs more than 6 times, and some destination occurs exactly 6 times.
All inputs are finite; a program needn't handle non-finite values.
Results may differ from a plain program's by a relative error of at most 0.0003.
Values may be sent and summed in bfloat16 or wider, within the bound.
A program may use at most 64 MiB of HBM per device.

v0:
```python
import jax
import jax.numpy as jnp
from jax import lax
from jax.sharding import PartitionSpec as P

OFFSETS = 8


FILTER_TAPS = (0.05, 0.08, 0.12, 0.15, 0.2, 0.15, 0.12, 0.08, 0.05)
dip_limit = 3
time_pad = 12


def padded_2(cells, sides, width):
    for axis, dim in sides:
        count = lax.axis_size(axis)
        ends = count - 1
        head = lax.slice_in_dim(cells, 0, width, axis=dim)
        tail = lax.slice_in_dim(cells, cells.shape[dim] - width, cells.shape[dim], axis=dim)
        cells = jnp.concatenate(
            [
                lax.ppermute(tail, axis, [(i, (i + 1) % count) for i in range(ends)]),
                cells,
                lax.ppermute(head, axis, [((i + 1) % count, i) for i in range(ends)]),
            ],
            axis=dim,
        )
    return cells


def dip_pass(padded, dips, axis, count, samples):
    running = None
    for tap_index in range(9):
        neighbour = lax.slice_in_dim(padded, tap_index, tap_index + count, axis=axis)
        shifted = jnp.zeros(neighbour.shape[:-1] + (samples,), jnp.float32)
        for dip_value in range(-dip_limit, dip_limit + 1):
            first_sample = time_pad + (tap_index - 4) * dip_value
            shifted = jnp.where(
                (dips == dip_value)[..., None],
                neighbour[..., first_sample : first_sample + samples],
                shifted,
            )
        term = FILTER_TAPS[tap_index] * shifted
        running = term if running is None else running + term
    return running


def per_device(traces, destination, bin_local, offset_class, dip_inline, dip_xline):
    n_inline = lax.axis_size("inline")
    n_xline = lax.axis_size("xline")
    devices = n_inline * n_xline
    row_count, samples = traces.shape
    capacity = 3 * row_count // devices
    inline_bins, xline_bins = dip_inline.shape
    bin_count = inline_bins * xline_bins
    target = destination[:, 0]
    matches = (target[:, None] == jnp.arange(devices, dtype=jnp.int32)[None, :]).astype(jnp.int32)
    before = jnp.cumsum(matches, axis=0) - matches
    position = jnp.sum(before * matches, axis=1)
    slot_index = target * capacity + position
    labels = offset_class * bin_count + bin_local
    outgoing = jnp.zeros((devices * capacity, samples), jnp.bfloat16).at[slot_index].set(traces)
    outgoing = outgoing.reshape(n_inline, n_xline, capacity, samples)
    out_labels = jnp.full((devices * capacity,), -1, jnp.int32).at[slot_index].set(labels)
    out_labels = out_labels.reshape(n_inline, n_xline, capacity)
    arrived, arrived_labels = (
        lax.all_to_all(
            lax.all_to_all(outgoing, "inline", split_axis=0, concat_axis=0, tiled=True),
            "xline",
            split_axis=1,
            concat_axis=1,
            tiled=True,
        ),
        lax.all_to_all(
            lax.all_to_all(out_labels, "inline", split_axis=0, concat_axis=0, tiled=True),
            "xline",
            split_axis=1,
            concat_axis=1,
            tiled=True,
        ),
    )
    received = arrived.reshape(-1, samples)
    got_labels = arrived_labels.reshape(-1)
    cell_total = OFFSETS * bin_count
    selector = jnp.arange(cell_total, dtype=jnp.int32)[:, None] == got_labels[None, :]
    totals = jnp.dot(selector.astype(jnp.bfloat16), received, preferred_element_type=jnp.float32)
    counts = jnp.sum(selector.astype(jnp.int32), axis=1).astype(jnp.float32)
    stacked = (totals / jnp.maximum(counts, 1.0)[:, None]).reshape(
        OFFSETS, inline_bins, xline_bins, samples
    )
    with_rim = padded_2(stacked, (("inline", 1),), 4)
    padded = jnp.pad(with_rim, ((0, 0), (0, 0), (0, 0), (time_pad, time_pad)))
    smoothed = dip_pass(padded, dip_inline, 1, inline_bins, samples)
    with_rim = padded_2(smoothed, (("xline", 2),), 4)
    padded = jnp.pad(with_rim, ((0, 0), (0, 0), (0, 0), (time_pad, time_pad)))
    return dip_pass(padded, dip_xline, 2, xline_bins, samples)


def solution(mesh):
    return jax.shard_map(
        per_device,
        mesh=mesh,
        in_specs=(
            P(("inline", "xline"), None),
            P(("inline", "xline"), None),
            P(("inline", "xline")),
            P(("inline", "xline")),
            P("inline", "xline"),
            P("inline", "xline"),
        ),
        out_specs=P(None, "inline", "xline", None),
        check_vma=False,
    )
```

profile of v0, /device:TPU:7, one launch (start us, length us, event | category | flops | bytes accessed | tf_op | source)
XLA Modules:
  0.0 310.8 jit_solution(10198870780576490040)
XLA Ops:
  0.0 0.9 copy.30
  1.6 2.5 scatter_custom_fusion
  4.0 0.8 reshape.35
  4.8 11.0 %all-to-all-start = ((s32[32,8,6]{2,1,0:T(8,128)}), s32[32,8,6]{2,1,0:T(8,128)S(1)}, u32[]{:S(2)}, u32[]{:S(2)}) async-start(s32[32,8,6]{2,1,0:T(8,128)} %reshape.35), calls=%async_computation | async-start | bytes 262144 | tf_op jit(solution)/shard_map/all_to_all | solution.py:75
  15.9 4.3 %scatter_custom_fusion.1 = bf16[1536,1024]{1,0:T(8,128)(2,1)S(1)} fusion(s32[512]{0:T(512)S(1)} %bitcast.35, bf16[512,1024]{1,0:T(8,128)(2,1)} %param.6, bf16[]{:T(256)} %constant.6.clone.1), kind=kCustom, calls=%fused_computation.183 | custom fusion | bytes 3146240 | tf_op jit(solution)/shard_map/scatter | solution.py:62
  20.2 2.9 reshape.36
  23.1 7.1 %copy.34 = bf16[32,8,6,1024]{3,1,2,0:T(8,128)(2,1)} copy(bf16[32,8,6,1024]{3,2,1,0:T(8,128)(2,1)} %reshape.36) | data formatting | bytes 6291456 | tf_op jit(solution)/shard_map/reshape | solution.py:63
  30.2 9.2 %all-to-all-start.2 = ((bf16[32,8,6,1024]{3,1,2,0:T(8,128)(2,1)}), bf16[32,8,6,1024]{3,1,2,0:T(8,128)(2,1)S(1)}, u32[]{:S(2)}, u32[]{:S(2)}) async-start(bf16[32,8,6,1024]{3,1,2,0:T(8,128)(2,1)} %copy.34), calls=%async_computation.2 | async-start | bytes 6291456 | tf_op jit(solution)/shard_map/all_to_all | solution.py:68
  40.2 68.5 %all-to-all-done.2 = bf16[32,8,6,1024]{3,1,2,0:T(8,128)(2,1)S(1)} async-done(((bf16[32,8,6,1024]{3,1,2,0:T(8,128)(2,1)}), bf16[32,8,6,1024]{3,1,2,0:T(8,128)(2,1)S(1)}, u32[]{:S(2)}, u32[]{:S(2)}) %all-to-all-start.2) | async-done | bytes 3145760 | tf_op jit(solution)/shard_map/all_to_all | solution.py:68
  108.8 9.0 %all-to-all-start.1 = ((s32[8,1,192]{2,1,0:T(1,128)}), s32[8,1,192]{2,1,0:T(1,128)S(1)}, u32[]{:S(2)}, u32[]{:S(2)}) async-start(s32[8,1,192]{2,1,0:T(1,128)} %reshape.59), calls=%async_computation.1 | async-start | bytes 16384 | tf_op jit(solution)/shard_map/all_to_all | solution.py:74
  117.7 3.4 %copy.35 = bf16[32,8,6,1024]{3,0,2,1:T(8,128)(2,1)} copy(bf16[32,8,6,1024]{3,1,2,0:T(8,128)(2,1)S(1)} %all-to-all-done.2) | data formatting | bytes 6291456 | tf_op jit(solution)/shard_map/all_to_all | solution.py:68
  121.1 1.2 all-to-all-done.1
  122.4 4.3 %all-to-all-start.3 = ((bf16[32,8,6,1024]{3,0,2,1:T(8,128)(2,1)}), bf16[32,8,6,1024]{3,0,2,1:T(8,128)(2,1)S(1)}, u32[]{:S(2)}, u32[]{:S(2)}) async-start(bf16[32,8,6,1024]{3,0,2,1:T(8,128)(2,1)} %copy.35), calls=%async_computation.3 | async-start | bytes 6291456 | tf_op jit(solution)/shard_map/all_to_all | solution.py:67
  128.6 35.6 %all-to-all-done.3 = bf16[32,8,6,1024]{3,0,2,1:T(8,128)(2,1)S(1)} async-done(((bf16[32,8,6,1024]{3,0,2,1:T(8,128)(2,1)}), bf16[32,8,6,1024]{3,0,2,1:T(8,128)(2,1)S(1)}, u32[]{:S(2)}, u32[]{:S(2)}) %all-to-all-start.3) | async-done | bytes 3145760 | tf_op jit(solution)/shard_map/all_to_all | solution.py:67
  164.2 3.7 %copy.36 = bf16[32,8,6,1024]{3,2,1,0:T(8,128)(2,1)} copy(bf16[32,8,6,1024]{3,0,2,1:T(8,128)(2,1)S(1)} %all-to-all-done.3) | data formatting | bytes 6291456 | tf_op jit(solution)/shard_map/all_to_all | solution.py:67
  167.9 4.9 %reshape.37 = bf16[1536,1024]{1,0:T(8,128)(2,1)S(1)} reshape(bf16[32,8,6,1024]{3,2,1,0:T(8,128)(2,1)} %copy.36) | data formatting | bytes 6291456 | tf_op jit(solution)/shard_map/reshape | solution.py:82
  172.8 1.8 fusion.142
  174.6 1.2 copy.37
  175.9 1.9 collective-permute-start
  177.8 5.7 %collective-permute-start.1 = (f32[8,4,16,1024]{3,0,2,1:T(8,128)S(1)}, f32[8,4,16,1024]{3,0,2,1:T(8,128)S(1)}, u32[]{:S(2)}, u32[]{:S(2)}) collective-permute-start(f32[8,4,16,1024]{3,0,2,1:T(8,128)S(1)} %copy.37), channel_id=1, source_target_pairs={{8,0},{16,8},{24,16},{32,24},{40,32},{48,40},{56,48},{64,56},{72,6... | collective-permute-start | bytes 6291464 | tf_op jit(solution)/shard_map/ppermute | solution.py:24
  183.5 42.6 %collective-permute-done = f32[8,4,16,1024]{3,0,2,1:T(8,128)S(1)} collective-permute-done((f32[8,4,16,1024]{3,0,2,1:T(8,128)S(1)}, f32[8,4,16,1024]{3,0,2,1:T(8,128)S(1)}, u32[]{:S(2)}, u32[]{:S(2)}) %collective-permute-start) | collective-permute-done | bytes 2097184 | tf_op jit(solution)/shard_map/ppermute | solution.py:22
  226.4 1.2 constant_dynamic-update-slice_fusion
  227.6 1.9 copy-done
  229.6 2.9 select_maximum_fusion
  232.7 28.2 %fusion.52 = f32[8,4,16,1024]{3,0,2,1:T(8,128)S(1)} fusion(f32[8,4,16,1024]{3,0,2,1:T(8,128)S(1)} %collective-permute-done.1, f32[8,12,16,1048]{3,0,2,1:T(8,128)S(1)} %select_maximum_fusion, f32[8,8,16,1024]{3,0,2,1:T(8,128)S(1)} %constant_dynamic-update-slice_fusion.2, f32[8,8,16,1024]{3,0,2,1:T(8,128)} %copy-done, ...), kind=kLoop, calls=%fused_computation.78 | loop fusion | flops 41943040 | bytes 121635264 | tf_op jit(solution)/shard_map/add | solution.py:44
  261.1 3.9 %collective-permute-start.2 = (f32[8,4,4,1024]{3,0,2,1:T(8,128)S(1)}, f32[8,4,4,1024]{3,0,2,1:T(8,128)S(1)}, u32[]{:S(2)}, u32[]{:S(2)}) collective-permute-start(f32[8,4,4,1024]{3,0,2,1:T(8,128)S(1)} %get-tuple-element.5), channel_id=1, source_target_pairs={{0,1},{1,2},{2,3},{3,4},{4,5},{5,6},{6,7},{8,9},{9,10},{10,11},{11... | collective-permute-start | bytes 1572872 | tf_op jit(solution)/shard_map/ppermute | solution.py:22
  265.0 2.2 collective-permute-start.3
  267.2 3.9 %collective-permute-done.2 = f32[8,4,4,1024]{3,0,2,1:T(8,128)S(1)} collective-permute-done((f32[8,4,4,1024]{3,0,2,1:T(8,128)S(1)}, f32[8,4,4,1024]{3,0,2,1:T(8,128)S(1)}, u32[]{:S(2)}, u32[]{:S(2)}) %collective-permute-start.2) | collective-permute-done | bytes 524320 | tf_op jit(solution)/shard_map/ppermute | solution.py:22
  271.1 4.4 %collective-permute-done.3 = f32[8,4,4,1024]{3,0,2,1:T(8,128)S(1)} collective-permute-done((f32[8,4,4,1024]{3,0,2,1:T(8,128)S(1)}, f32[8,4,4,1024]{3,0,2,1:T(8,128)S(1)}, u32[]{:S(2)}, u32[]{:S(2)}) %collective-permute-start.3) | collective-permute-done | bytes 524320 | tf_op jit(solution)/shard_map/ppermute | solution.py:24
  275.5 1.0 select_maximum_fusion.2
  276.4 31.8 %fusion.10 = f32[8,4,16,1024]{3,0,2,1:T(8,128)S(1)} fusion(f32[8,4,16,1024]{3,0,2,1:T(8,128)S(1)} %fusion.52, f32[8,4,4,1024]{3,0,2,1:T(8,128)S(1)} %collective-permute-done.3, f32[8,4,4,1024]{3,0,2,1:T(8,128)S(1)} %collective-permute-done.2, f32[8,4,24,1048]{3,0,2,1:T(8,128)S(1)} %select_maximum_fusion.2, pred[4,16]{1,0:T(4,128)(4,1)S(1)} %get-tuple-element.14, ...), kind=kLoop, calls=%fused_computation.36 | loop fusion | flops 46137344 | bytes 105906624 | tf_op jit(solution)/shard_map/add | solution.py:44
  308.2 2.5 copy.49
  (37 shorter events, 4.0 us)
Async XLA Ops:
  0.0 1.3 copy-start.1
  0.0 1.5 copy-start.3
  0.0 1.5 copy-start.2
  4.8 25.4 %all-to-all-start = ((s32[32,8,6]{2,1,0:T(8,128)}), s32[32,8,6]{2,1,0:T(8,128)S(1)}, u32[]{:S(2)}, u32[]{:S(2)}) async-start(s32[32,8,6]{2,1,0:T(8,128)} %reshape.35), calls=%async_computation | async-start | bytes 262144 | tf_op jit(solution)/shard_map/all_to_all | solution.py:75
  30.2 78.6 %all-to-all-start.2 = ((bf16[32,8,6,1024]{3,1,2,0:T(8,128)(2,1)}), bf16[32,8,6,1024]{3,1,2,0:T(8,128)(2,1)S(1)}, u32[]{:S(2)}, u32[]{:S(2)}) async-start(bf16[32,8,6,1024]{3,1,2,0:T(8,128)(2,1)} %copy.34), calls=%async_computation.2 | async-start | bytes 6291456 | tf_op jit(solution)/shard_map/all_to_all | solution.py:68
  108.8 13.6 %all-to-all-start.1 = ((s32[8,1,192]{2,1,0:T(1,128)}), s32[8,1,192]{2,1,0:T(1,128)S(1)}, u32[]{:S(2)}, u32[]{:S(2)}) async-start(s32[8,1,192]{2,1,0:T(1,128)} %reshape.59), calls=%async_computation.1 | async-start | bytes 16384 | tf_op jit(solution)/shard_map/all_to_all | solution.py:74
  122.4 41.8 %all-to-all-start.3 = ((bf16[32,8,6,1024]{3,0,2,1:T(8,128)(2,1)}), bf16[32,8,6,1024]{3,0,2,1:T(8,128)(2,1)S(1)}, u32[]{:S(2)}, u32[]{:S(2)}) async-start(bf16[32,8,6,1024]{3,0,2,1:T(8,128)(2,1)} %copy.35), calls=%async_computation.3 | async-start | bytes 6291456 | tf_op jit(solution)/shard_map/all_to_all | solution.py:67
  174.6 8.9 %copy-start.4 = (s32[4,16]{1,0:T(4,128)S(1)}, s32[4,16]{1,0:T(4,128)}, u32[]{:S(2)}) copy-start(s32[4,16]{1,0:T(4,128)} %param.10) | copy-start | bytes 772
  175.9 50.3 %collective-permute-start = (f32[8,4,16,1024]{3,0,2,1:T(8,128)S(1)}, f32[8,4,16,1024]{3,0,2,1:T(8,128)S(1)}, u32[]{:S(2)}, u32[]{:S(2)}) collective-permute-start(f32[8,4,16,1024]{3,0,2,1:T(8,128)S(1)} %copy.37), channel_id=1, source_target_pairs={{0,8},{8,16},{16,24},{24,32},{32,40},{40,48},{48,56},{56,64},{64,7... | collective-permute-start | bytes 6291464 | tf_op jit(solution)/shard_map/ppermute | solution.py:22
  177.8 51.8 %collective-permute-start.1 = (f32[8,4,16,1024]{3,0,2,1:T(8,128)S(1)}, f32[8,4,16,1024]{3,0,2,1:T(8,128)S(1)}, u32[]{:S(2)}, u32[]{:S(2)}) collective-permute-start(f32[8,4,16,1024]{3,0,2,1:T(8,128)S(1)} %copy.37), channel_id=1, source_target_pairs={{8,0},{16,8},{24,16},{32,24},{40,32},{48,40},{56,48},{64,56},{72,6... | collective-permute-start | bytes 6291464 | tf_op jit(solution)/shard_map/ppermute | solution.py:24
  227.6 1.9 copy-start
  261.0 6.2 %copy-start.5 = (s32[4,16]{1,0:T(4,128)S(1)}, s32[4,16]{1,0:T(4,128)}, u32[]{:S(2)}) copy-start(s32[4,16]{1,0:T(4,128)} %param.11) | copy-start | bytes 772
  261.1 10.0 %collective-permute-start.2 = (f32[8,4,4,1024]{3,0,2,1:T(8,128)S(1)}, f32[8,4,4,1024]{3,0,2,1:T(8,128)S(1)}, u32[]{:S(2)}, u32[]{:S(2)}) collective-permute-start(f32[8,4,4,1024]{3,0,2,1:T(8,128)S(1)} %get-tuple-element.5), channel_id=1, source_target_pairs={{0,1},{1,2},{2,3},{3,4},{4,5},{5,6},{6,7},{8,9},{9,10},{10,11},{11... | collective-permute-start | bytes 1572872 | tf_op jit(solution)/shard_map/ppermute | solution.py:22
  265.0 10.5 %collective-permute-start.3 = (f32[8,4,4,1024]{3,0,2,1:T(8,128)S(1)}, f32[8,4,4,1024]{3,0,2,1:T(8,128)S(1)}, u32[]{:S(2)}, u32[]{:S(2)}) collective-permute-start(f32[8,4,4,1024]{3,0,2,1:T(8,128)S(1)} %get-tuple-element.6), channel_id=1, source_target_pairs={{1,0},{2,1},{3,2},{4,3},{5,4},{6,5},{7,6},{9,8},{10,9},{11,10},{12... | collective-permute-start | bytes 1572872 | tf_op jit(solution)/shard_map/ppermute | solution.py:24
where the time goes:
time: 311 us
  waiting for transfers between devices  156 us (50%)
  other arithmetic  65.5 us (21%)
  starting transfers between devices  47.2 us (15%)
  local copies, waits for them, and re-layouts  39.7 us (13%)
    all_to_all x1, waiting for transfers between devices, per_device(): lax.all_to_all(outgoing, 'inline', split_axis=0, concat_axis=0, tiled=True)  68.5 us
    add x2, other arithmetic, dip_pass(): running = term if running is None else running + term  60 us
    ppermute x2, waiting for transfers between devices, padded_2(): lax.ppermute(tail, axis, [(i, (i + 1) % count) for i in range(ends)])  46.5 us
    all_to_all x1, waiting for transfers between devices, per_device(): lax.all_to_all(lax.all_to_all(outgoing, 'inline', split_axis=0, concat_ax...  35.6 us
    all_to_all x1, starting transfers between devices, per_device(): lax.all_to_all(out_labels, 'inline', split_axis=0, concat_axis=0, tiled=T...  11 us
    reshape x2, local copies, waits for them, and re-layouts, per_device(): outgoing = outgoing.reshape(n_inline, n_xline, capacity, samples)  9.98 us
    all_to_all x1, starting transfers between devices, per_device(): lax.all_to_all(outgoing, 'inline', split_axis=0, concat_axis=0, tiled=True)  9.23 us
    all_to_all x1, starting transfers between devices, per_device(): lax.all_to_all(lax.all_to_all(out_labels, 'inline', split_axis=0, concat_...  8.99 us
  transfers between devices with their start and end apart: 8, of which 6 were waited for; matrix products, arithmetic and copies ran while one was open for 7% of the time, Pallas kernels for 0%

commit v1 on v0

--- a/solution.py
+++ b/solution.py
@@ -1,14 +1,387 @@
 import jax
 import jax.numpy as jnp
 from jax import lax
+from jax.experimental import pallas as pl
+from jax.experimental.pallas import tpu as pltpu
 from jax.sharding import PartitionSpec as P
 
 OFFSETS = 8
-
-
 FILTER_TAPS = (0.05, 0.08, 0.12, 0.15, 0.2, 0.15, 0.12, 0.08, 0.05)
 dip_limit = 3
 time_pad = 12
+
+MESH = pl.DeviceIdType.MESH
+N_Z = 8
+N_P = 32
+N_XL = 8
+CAP = 6
+POOL = 96
+SLOTS = N_Z * CAP
+ROWS = N_P * SLOTS
+CELLS = 512
+T = 4
+NT = (((1,), (1,)), ((), ()))
+f32, bf16, i32 = jnp.float32, jnp.bfloat16, jnp.int32
+
+
+def iota(shape, dim):
+    return lax.broadcasted_iota(i32, shape, dim)
+
+
+def onehot(mask):
+    return jnp.where(mask, 1.0, 0.0).astype(bf16)
+
+
+def route_kernel(
+    traces, dest, bins, offs, stacked, flag_out,
+    rows, p1, send1, recv1, lab1s, lab1r, l2, p2, send2, recv2, lab2s, lab2r, wide, sel, count,
+    s1_send, s1_recv, l1_send, l1_recv, s2_send, s2_recv, l2_send, l2_recv,
+):
+    n, samples = traces.shape
+    w = samples // T
+    me_i = lax.axis_index("inline")
+    me_x = lax.axis_index("xline")
+    my_z = lax.rem(me_i, N_Z)
+    my_col = me_i // N_Z
+    my_p = my_col * N_XL + me_x
+
+    def z_peer(k):
+        z = lax.rem(my_z + k, N_Z)
+        return z, (my_col * N_Z + z, me_x)
+
+    def p_peer(k):
+        p = lax.rem(my_p + k, N_P)
+        return p, ((p // N_XL) * N_Z + my_z, lax.rem(p, N_XL))
+
+    barrier = pltpu.get_barrier_semaphore()
+
+    @pl.loop(1, N_Z)
+    def _(k):
+        pl.semaphore_signal(barrier, inc=1, device_id=z_peer(k)[1], device_id_type=MESH)
+
+    @pl.loop(1, N_P)
+    def _(k):
+        pl.semaphore_signal(barrier, inc=1, device_id=p_peer(k)[1], device_id_type=MESH)
+
+    d = dest[...]
+    eye = onehot(iota((n, n), 0) == iota((n, n), 1))
+    wide_d = jnp.broadcast_to(d.astype(f32), (128, n)).astype(bf16)
+    dcol = lax.dot_general(eye, wide_d, NT, preferred_element_type=f32).astype(i32)
+    zcol = (dcol >> 3) & 7
+    for t in range(n // 128):
+        lanes = slice(t * 128, (t + 1) * 128)
+        drow = d[:, lanes]
+        earlier = iota((n, 128), 0) < iota((n, 128), 1) + t * 128
+        same = (dcol == drow) & earlier
+        same_z = (zcol == ((drow >> 3) & 7)) & earlier
+        rows[0:1, lanes] = jnp.sum(jnp.where(same, 1.0, 0.0), axis=0, keepdims=True)
+        rows[1:2, lanes] = jnp.sum(jnp.where(same_z, 1.0, 0.0), axis=0, keepdims=True)
+    position = rows[0:1, :].astype(i32)
+    place = rows[1:2, :].astype(i32)
+    zrow = (d >> 3) & 7
+    plane = (d >> 6) * N_XL + (d & 7)
+    over = jnp.max(place, axis=1, keepdims=True) >= POOL
+    over = jnp.where(over, 1, 0)
+    sub = iota((16, n), 0)
+    labels = jnp.where(sub == 0, plane, 0)
+    labels = jnp.where(sub == 1, my_z * CAP + position + 1, labels)
+    labels = jnp.where(sub == 2, bins[...], labels)
+    labels = jnp.where(sub == 3, offs[...], labels)
+    labels = labels.astype(f32).astype(bf16)
+
+    @pl.loop(0, N_Z)
+    def _(z):
+        target = jnp.where(zrow == z, place, -1)
+        pick = onehot(iota((128, n), 0) == target)
+        p1[z] = pick
+        lab = lax.dot_general(labels, pick, NT, preferred_element_type=f32)[:8].astype(i32)
+        lab = jnp.where(iota((8, 128), 1) < POOL, lab, 0)
+        lab1s[z] = jnp.where(iota((8, 128), 0) == 4, over, lab)
+
+    lab1r[my_z] = lab1s[my_z]
+
+    @pl.loop(0, T * N_Z)
+    def _(i):
+        recv1[i // N_Z, lax.rem(i, N_Z), POOL:, :] = jnp.zeros((128 - POOL, w), bf16)
+
+    pl.semaphore_wait(barrier, N_Z - 1 + N_P - 1)
+
+    def lab1_copy(k):
+        z, peer = z_peer(k)
+        return pltpu.make_async_remote_copy(
+            src_ref=lab1s.at[z], dst_ref=lab1r.at[my_z],
+            send_sem=l1_send.at[k], recv_sem=l1_recv.at[k],
+            device_id=peer, device_id_type=MESH,
+        )
+
+    def row1_copy(t, k):
+        z, peer = z_peer(k)
+        return pltpu.make_async_remote_copy(
+            src_ref=send1.at[t, z], dst_ref=recv1.at[t, my_z, pl.ds(0, POOL), :],
+            send_sem=s1_send.at[t, k], recv_sem=s1_recv.at[t, k],
+            device_id=peer, device_id_type=MESH,
+        )
+
+    def lab2_copy(k):
+        p, peer = p_peer(k)
+        return pltpu.make_async_remote_copy(
+            src_ref=lab2s.at[p], dst_ref=lab2r.at[my_p],
+            send_sem=l2_send.at[k], recv_sem=l2_recv.at[k],
+            device_id=peer, device_id_type=MESH,
+        )
+
+    def row2_copy(t, k):
+        p, peer = p_peer(k)
+        return pltpu.make_async_remote_copy(
+            src_ref=send2.at[t, p], dst_ref=recv2.at[t, my_p],
+            send_sem=s2_send.at[t, k], recv_sem=s2_recv.at[t, k],
+            device_id=peer, device_id_type=MESH,
+        )
+
+    @pl.loop(1, N_Z)
+    def _(k):
+        lab1_copy(k).start()
+
+    for t in range(T):
+        cols = slice(t * w, (t + 1) * w)
+
+        def picked(z, cols=cols):
+            return jnp.dot(p1[z][:POOL], traces[:, cols], preferred_element_type=f32).astype(bf16)
+
+        @pl.loop(1, N_Z)
+        def _(k, t=t, picked=picked):
+            z, _peer = z_peer(k)
+            send1[t, z] = picked(z)
+            row1_copy(t, k).start()
+
+        recv1[t, my_z, 0:POOL, :] = picked(my_z)
+
+    @pl.loop(1, N_Z)
+    def _(k):
+        lab1_copy(k).wait()
+
+    def seen(z, worst):
+        lab = lab1r[z]
+        code = lab[1:2, :]
+        target = jnp.where(code > 0, lab[0:1, :] * SLOTS + code - 1, -1)
+        lanes = pl.ds(pl.multiple_of(z * 128, 128), 128)
+        p2[:, lanes] = onehot(iota((ROWS, 128), 0) == target)
+        l2[:, lanes] = jnp.concatenate([lab, lab], axis=0).astype(f32).astype(bf16)
+        return jnp.maximum(worst, lab[4:5, :])
+
+    worst = lax.fori_loop(0, N_Z, seen, jnp.zeros((1, 128), i32))
+    lab = lax.dot_general(l2[...], p2[...], NT, preferred_element_type=f32).astype(i32)
+    cell = jnp.where(lab[1:2, :] > 0, lab[2:3, :] * OFFSETS + lab[3:4, :], -1)
+    wide[...] = jnp.where(iota((8, ROWS), 0) == 1, worst[:, 0:1], cell)
+
+    @pl.loop(0, N_P // 8)
+    def _(g):
+        part = wide[:, pl.ds(pl.multiple_of(g * 8 * SLOTS, 128), 8 * SLOTS)]
+        for i in range(8):
+            lab2s[g * 8 + i, :, 0:SLOTS] = part[:, i * SLOTS:(i + 1) * SLOTS]
+
+    lab2r[my_p] = lab2s[my_p]
+
+    @pl.loop(1, N_P)
+    def _(k):
+        lab2_copy(k).start()
+
+    def forward(t):
+        @pl.loop(1, N_Z)
+        def _(k):
+            row1_copy(t, k).wait()
+
+        arrived = recv1[t].reshape(N_Z * 128, w)
+
+        @pl.loop(0, N_P // 8)
+        def _(g):
+            pick = p2[pl.ds(pl.multiple_of(g * 8 * SLOTS, 128), 8 * SLOTS), :]
+            out = jnp.dot(pick, arrived, preferred_element_type=f32).astype(bf16)
+            send2[t, pl.ds(g * 8, 8)] = out.reshape(8, SLOTS, w)
+
+        @pl.loop(1, N_P)
+        def _(k):
+            row2_copy(t, k).start()
+
+        recv2[t, my_p] = send2[t, my_p]
+
+    def selector():
+        @pl.loop(1, N_P)
+        def _(k):
+            lab2_copy(k).wait()
+
+        @pl.loop(0, N_P // 8)
+        def _(g):
+            part = jnp.concatenate([lab2r[g * 8 + i][:, 0:SLOTS] for i in range(8)], axis=1)
+            wide[:, pl.ds(pl.multiple_of(g * 8 * SLOTS, 128), 8 * SLOTS)] = part
+
+        @pl.loop(0, ROWS // 128)
+        def _(c):
+            lanes = pl.ds(pl.multiple_of(c * 128, 128), 128)
+            sel[:, lanes] = onehot(iota((CELLS, 128), 0) == wide[0:1, lanes])
+
+        traces_per_cell = jnp.dot(sel[...], jnp.ones((ROWS, 128), bf16), preferred_element_type=f32)
+        count[...] = jnp.maximum(traces_per_cell, 1.0)
+        flag_out[...] = jnp.broadcast_to(jnp.max(wide[1:2, :], axis=1, keepdims=True), (8, 128))
+
+    def stack(t):
+        @pl.loop(1, N_P)
+        def _(k):
+            row2_copy(t, k).wait()
+
+        total = jnp.dot(sel[...], recv2[t].reshape(ROWS, w), preferred_element_type=f32)
+        for c in range(w // 128):
+            stacked[:, t * w + c * 128:t * w + (c + 1) * 128] = total[:, c * 128:(c + 1) * 128] / count[...]
+
+    for t in range(T):
+        forward(t)
+        if t == 0:
+            selector()
+        if t > 0:
+            stack(t - 1)
+    stack(T - 1)
+
+
+def route(traces, dest, bins, offs):
+    n, samples = traces.shape
+    w = samples // T
+    vmem = pl.BlockSpec(memory_space=pltpu.VMEM)
+    dma = pltpu.SemaphoreType.DMA
+    return pl.pallas_call(
+        route_kernel,
+        out_shape=(
+            jax.ShapeDtypeStruct((CELLS, samples), f32),
+            jax.ShapeDtypeStruct((8, 128), i32),
+        ),
+        in_specs=[vmem] * 4,
+        out_specs=(vmem, vmem),
+        scratch_shapes=[
+            pltpu.VMEM((8, n), f32),
+            pltpu.VMEM((N_Z, 128, n), bf16),
+            pltpu.VMEM((T, N_Z, POOL, w), bf16),
+            pltpu.VMEM((T, N_Z, 128, w), bf16),
+            pltpu.VMEM((N_Z, 8, 128), i32),
+            pltpu.VMEM((N_Z, 8, 128), i32),
+            pltpu.VMEM((16, N_Z * 128), bf16),
+            pltpu.VMEM((ROWS, N_Z * 128), bf16),
+            pltpu.VMEM((T, N_P, SLOTS, w), bf16),
+            pltpu.VMEM((T, N_P, SLOTS, w), bf16),
+            pltpu.VMEM((N_P, 8, 128), i32),
+            pltpu.VMEM((N_P, 8, 128), i32),
+            pltpu.VMEM((8, ROWS), i32),
+            pltpu.VMEM((CELLS, ROWS), bf16),
+            pltpu.VMEM((CELLS, 128), f32),
+            dma((T, N_Z)), dma((T, N_Z)), dma((N_Z,)), dma((N_Z,)),
+            dma((T, N_P)), dma((T, N_P)), dma((N_P,)), dma((N_P,)),
+        ],
+        compiler_params=pltpu.CompilerParams(
+            collective_id=0, has_side_effects=True, vmem_limit_bytes=48 * 1024 * 1024
+        ),
+    )(traces, dest, bins, offs)
+
+
+def steer(blocks, dip):
+    samples = blocks(0).shape[1]
+    parts = samples // 128
+    lane = iota((8, 128), 1)
+
+    def signed(up):
+        acc = [FILTER_TAPS[4] * blocks(0)[:, k * 128:(k + 1) * 128] for k in range(parts)]
+        zero = jnp.zeros((8, 128), f32)
+        for j in (-4, -3, -2, -1, 1, 2, 3, 4):
+            shift = j * dip
+            block = blocks(j)
+            turn = lax.rem(128 - shift, 128)
+            turned = [pltpu.roll(block[:, k * 128:(k + 1) * 128], turn, 1) for k in range(parts)]
+            if up == (j > 0):
+                keep = lane < 128 - shift
+                other = turned[1:] + [zero]
+            else:
+                keep = lane >= -shift
+                other = [zero] + turned[:-1]
+            for k in range(parts):
+                acc[k] += FILTER_TAPS[j + 4] * jnp.where(keep, turned[k], other[k])
+        return acc
+
+    return lax.cond(dip >= 0, lambda: signed(True), lambda: signed(False))
+
+
+def inline_kernel(dips, before, own, after, out):
+    n_il, n_xl = own.shape[0], own.shape[1]
+    base = pl.program_id(0) * n_xl
+
+    @pl.loop(0, n_xl)
+    def _(x):
+        for i in range(n_il):
+            def blocks(j, i=i):
+                at = i + j
+                ref = before if at < 0 else own if at < n_il else after
+                return ref[at % n_il, x]
+
+            acc = steer(blocks, dips[i, base + x])
+            for k, part in enumerate(acc):
+                out[i, x, :, k * 128:(k + 1) * 128] = part
+
+
+def inline_pass(dips, before, own, after):
+    n_il, n_xl, _, samples = own.shape
+    step = 4
+    block = pl.BlockSpec((n_il, step, OFFSETS, samples), lambda s: (0, s, 0, 0))
+    return pl.pallas_call(
+        inline_kernel,
+        grid=(n_xl // step,),
+        out_shape=jax.ShapeDtypeStruct(own.shape, f32),
+        in_specs=[pl.BlockSpec(memory_space=pltpu.SMEM), block, block, block],
+        out_specs=block,
+        compiler_params=pltpu.CompilerParams(vmem_limit_bytes=32 * 1024 * 1024),
+    )(dips, before, own, after)
+
+
+def xline_kernel(dips, left, own, right, out, ext, turned):
+    n_xl = own.shape[1]
+    il = pl.program_id(0)
+    ext[0:4] = left[0]
+    ext[4:4 + n_xl] = own[0]
+    ext[4 + n_xl:] = right[0]
+
+    @pl.loop(0, n_xl)
+    def _(x):
+        acc = steer(lambda j: ext[x + 4 + j], dips[il, x])
+        for k, part in enumerate(acc):
+            turned[k, pl.ds(x, OFFSETS, stride=n_xl), :] = part
+
+    for k in range(turned.shape[0]):
+        out[:, 0, :, k * 128:(k + 1) * 128] = turned[k].reshape(OFFSETS, n_xl, 128)
+
+
+def xline_pass(dips, left, own, right):
+    n_il, n_xl, _, samples = own.shape
+    side = pl.BlockSpec((1, 4, OFFSETS, samples), lambda s: (s, 0, 0, 0))
+    return pl.pallas_call(
+        xline_kernel,
+        grid=(n_il,),
+        out_shape=jax.ShapeDtypeStruct((OFFSETS, n_il, n_xl, samples), f32),
+        in_specs=[
+            pl.BlockSpec(memory_space=pltpu.SMEM),
+            side,
+            pl.BlockSpec((1, n_xl, OFFSETS, samples), lambda s: (s, 0, 0, 0)),
+            side,
+        ],
+        out_specs=pl.BlockSpec((OFFSETS, 1, n_xl, samples), lambda s: (0, s, 0, 0)),
+        scratch_shapes=[
+            pltpu.VMEM((n_xl + 8, OFFSETS, samples), f32),
+            pltpu.VMEM((samples // 128, OFFSETS * n_xl, 128), f32),
+        ],
+        compiler_params=pltpu.CompilerParams(vmem_limit_bytes=32 * 1024 * 1024),
+    )(dips, left, own, right)
+
+
+def shifted(cells, axis):
+    count = lax.axis_size(axis)
+    return (
+        lambda tail: lax.ppermute(tail, axis, [(i, i + 1) for i in range(count - 1)]),
+        lambda head: lax.ppermute(head, axis, [(i + 1, i) for i in range(count - 1)]),
+    )
 
 
 def padded_2(cells, sides, width):
@@ -32,20 +405,20 @@
     running = None
     for tap_index in range(9):
         neighbour = lax.slice_in_dim(padded, tap_index, tap_index + count, axis=axis)
-        shifted = jnp.zeros(neighbour.shape[:-1] + (samples,), jnp.float32)
+        moved = jnp.zeros(neighbour.shape[:-1] + (samples,), jnp.float32)
         for dip_value in range(-dip_limit, dip_limit + 1):
             first_sample = time_pad + (tap_index - 4) * dip_value
-            shifted = jnp.where(
+            moved = jnp.where(
                 (dips == dip_value)[..., None],
                 neighbour[..., first_sample : first_sample + samples],
-                shifted,
+                moved,
             )
-        term = FILTER_TAPS[tap_index] * shifted
+        term = FILTER_TAPS[tap_index] * moved
         running = term if running is None else running + term
     return running
 
 
-def per_device(traces, destination, bin_local, offset_class, dip_inline, dip_xline):
+def any_load(traces, destination, bin_local, offset_class, dip_inline, dip_xline):
     n_inline = lax.axis_size("inline")
     n_xline = lax.axis_size("xline")
     devices = n_inline * n_xline
@@ -63,24 +436,13 @@
     outgoing = outgoing.reshape(n_inline, n_xline, capacity, samples)
     out_labels = jnp.full((devices * capacity,), -1, jnp.int32).at[slot_index].set(labels)
     out_labels = out_labels.reshape(n_inline, n_xline, capacity)
-    arrived, arrived_labels = (
-        lax.all_to_all(
-            lax.all_to_all(outgoing, "inline", split_axis=0, concat_axis=0, tiled=True),
-            "xline",
-            split_axis=1,
-            concat_axis=1,
-            tiled=True,
-        ),
-        lax.all_to_all(
-            lax.all_to_all(out_labels, "inline", split_axis=0, concat_axis=0, tiled=True),
-            "xline",
-            split_axis=1,
-            concat_axis=1,
-            tiled=True,
-        ),
-    )
-    received = arrived.reshape(-1, samples)
-    got_labels = arrived_labels.reshape(-1)
+
+    def exchange(value):
+        value = lax.all_to_all(value, "inline", split_axis=0, concat_axis=0, tiled=True)
+        return lax.all_to_all(value, "xline", split_axis=1, concat_axis=1, tiled=True)
+
+    received = exchange(outgoing).reshape(-1, samples)
+    got_labels = exchange(out_labels).reshape(-1)
     cell_total = OFFSETS * bin_count
     selector = jnp.arange(cell_total, dtype=jnp.int32)[:, None] == got_labels[None, :]
     totals = jnp.dot(selector.astype(jnp.bfloat16), received, preferred_element_type=jnp.float32)
@@ -94,6 +456,25 @@
     with_rim = padded_2(smoothed, (("xline", 2),), 4)
     padded = jnp.pad(with_rim, ((0, 0), (0, 0), (0, 0), (time_pad, time_pad)))
     return dip_pass(padded, dip_xline, 2, xline_bins, samples)
+
+
+def per_device(traces, destination, bin_local, offset_class, dip_inline, dip_xline):
+    n, samples = traces.shape
+    n_il, n_xl = dip_inline.shape
+    stacked, flag = route(
+        traces, destination.reshape(1, n), bin_local.reshape(1, n), offset_class.reshape(1, n)
+    )
+    stacked = stacked.reshape(n_il, n_xl, OFFSETS, samples)
+    up, down = shifted(stacked, "inline")
+    first = inline_pass(dip_inline, up(stacked), stacked, down(stacked))
+    right, left = shifted(first, "xline")
+    from_left = right(first[:, n_xl - 4:])
+    from_right = left(first[:, :4])
+    return lax.cond(
+        flag[0, 0] > 0,
+        lambda: any_load(traces, destination, bin_local, offset_class, dip_inline, dip_xline),
+        lambda: xline_pass(dip_xline, from_left, first, from_right),
+    )
 
 
 def solution(mesh):

time: 311 us -> 169 us (0.54)
  the two profiles are of different devices: /device:TPU:7 before, /device:TPU:49 now
where the time goes in v1:
time: 169 us
  Pallas kernels  85.9 us (51%)
  waiting for transfers between devices  63.5 us (38%)
  starting transfers between devices  17.9 us (11%)
    pallas_call x1, Pallas kernels, route(): pl.pallas_call(route_kernel, out_shape=(jax.ShapeDtypeStruct((CELLS, samp...  63.4 us
    ppermute x2, waiting for transfers between devices, shifted(): lax.ppermute(tail, axis, [(i, i + 1) for i in range(count - 1)])  45.7 us
    ppermute x2, waiting for transfers between devices, shifted(): lax.ppermute(head, axis, [(i + 1, i) for i in range(count - 1)])  17.9 us
    ppermute x2, starting transfers between devices, shifted(): lax.ppermute(tail, axis, [(i, i + 1) for i in range(count - 1)])  14 us
    pallas_call x1, Pallas kernels, xline_pass(): pl.pallas_call(xline_kernel, grid=(n_il,), out_shape=jax.ShapeDtypeStruct...  11.9 us
    pallas_call x1, Pallas kernels, inline_pass(): pl.pallas_call(inline_kernel, grid=(n_xl // step,), out_shape=jax.ShapeDt...  10.5 us
    ppermute x2, starting transfers between devices, shifted(): lax.ppermute(head, axis, [(i + 1, i) for i in range(count - 1)])  3.84 us
  transfers between devices with their start and end apart: 4, of which 4 were waited for; matrix products, arithmetic and copies ran while one was open for 0% of the time, Pallas kernels for 0%

profile of v1, /device:TPU:49, one launch (start us, length us, event | category | flops | bytes accessed | tf_op | source)
XLA Modules:
  0.0 168.7 jit_solution(13204475916973583312)
XLA Ops:
  0.0 63.4 %shard_map.66 = (f32[512,1024]{1,0:T(8,128)S(1)}, s32[8,128]{1,0:T(8,128)S(1)}) custom-call(bf16[512,1024]{1,0:T(8,128)(2,1)} %traces.1, s32[1,512]{1,0:T(1,128)} %bitcast.37, s32[1,512]{1,0:T(1,128)} %bitcast.41, s32[1,512]{1,0:T(1,128)} %bitcast.42), custom_call_target="tpu_custom_call" | custom-call | tf_op jit(solution)/shard_map/pallas_call | solution.py:250
  63.5 9.6 %collective-permute-start.4 = (f32[4,16,8,1024]{3,2,1,0:T(8,128)S(1)}, f32[4,16,8,1024]{3,2,1,0:T(8,128)S(1)}, u32[]{:S(2)}, u32[]{:S(2)}) collective-permute-start(f32[4,16,8,1024]{3,2,1,0:T(8,128)S(1)} %bitcast.26), channel_id=1, source_target_pairs={{0,8},{8,16},{16,24},{24,32},{32,40},{40,48},{48,56},{56,64},{64,7... | collective-permute-start | bytes 6291464 | tf_op jit(solution)/shard_map/ppermute | solution.py:382
  73.1 1.9 %collective-permute-start.5 = (f32[4,16,8,1024]{3,2,1,0:T(8,128)S(1)}, f32[4,16,8,1024]{3,2,1,0:T(8,128)S(1)}, u32[]{:S(2)}, u32[]{:S(2)}) collective-permute-start(f32[4,16,8,1024]{3,2,1,0:T(8,128)S(1)} %bitcast.27), channel_id=1, source_target_pairs={{8,0},{16,8},{24,16},{32,24},{40,32},{48,40},{56,48},{64,56},{72,6... | collective-permute-start | bytes 6291464 | tf_op jit(solution)/shard_map/ppermute | solution.py:383
  75.0 42.7 %collective-permute-done.4.before = f32[4,16,8,1024]{3,2,1,0:T(8,128)S(1)} collective-permute-done((f32[4,16,8,1024]{3,2,1,0:T(8,128)S(1)}, f32[4,16,8,1024]{3,2,1,0:T(8,128)S(1)}, u32[]{:S(2)}, u32[]{:S(2)}) %collective-permute-start.4) | collective-permute-done | bytes 2097184 | tf_op jit(solution)/shard_map/ppermute | solution.py:382
  117.7 13.5 %collective-permute-done.5.after = f32[4,16,8,1024]{3,2,1,0:T(8,128)S(1)} collective-permute-done((f32[4,16,8,1024]{3,2,1,0:T(8,128)S(1)}, f32[4,16,8,1024]{3,2,1,0:T(8,128)S(1)}, u32[]{:S(2)}, u32[]{:S(2)}) %collective-permute-start.5) | collective-permute-done | bytes 2097184 | tf_op jit(solution)/shard_map/ppermute | solution.py:383
  131.1 10.5 %shard_map.67 = f32[4,16,8,1024]{3,2,1,0:T(8,128)S(1)} custom-call(s32[4,16]{1,0:T(4,128)} %dips.1, f32[4,16,8,1024]{3,2,1,0:T(8,128)S(1)} %collective-permute-done.4.before, f32[4,16,8,1024]{3,2,1,0:T(8,128)S(1)} %bitcast.28, f32[4,16,8,1024]{3,2,1,0:T(8,128)S(1)} %collective-permute-done.5.after), custom_call_target="tpu_custom_call" | custom-call | tf_op jit(solution)/shard_map/pallas_call | solution.py:330
  141.6 0.0 copy-start
  141.7 0.0 copy-start.1
  141.7 0.0 copy-start.2
  141.7 0.0 copy-start.3
  141.7 0.0 copy-start.4
  141.7 0.1 fusion.155
  141.8 4.4 %collective-permute-start.6 = (f32[4,4,8,1024]{3,2,1,0:T(8,128)S(1)}, f32[4,4,8,1024]{3,2,1,0:T(8,128)S(1)}, u32[]{:S(2)}, u32[]{:S(2)}) collective-permute-start(f32[4,4,8,1024]{3,2,1,0:T(8,128)S(1)} %get-tuple-element.60), channel_id=1, source_target_pairs={{0,1},{1,2},{2,3},{3,4},{4,5},{5,6},{6,7},{8,9},{9,10},{10,11},{11... | collective-permute-start | bytes 1572872 | tf_op jit(solution)/shard_map/ppermute | solution.py:382
  146.2 1.9 %collective-permute-start.7 = (f32[4,4,8,1024]{3,2,1,0:T(8,128)S(1)}, f32[4,4,8,1024]{3,2,1,0:T(8,128)S(1)}, u32[]{:S(2)}, u32[]{:S(2)}) collective-permute-start(f32[4,4,8,1024]{3,2,1,0:T(8,128)S(1)} %get-tuple-element.59), channel_id=1, source_target_pairs={{1,0},{2,1},{3,2},{4,3},{5,4},{6,5},{7,6},{9,8},{10,9},{11,10},{12... | collective-permute-start | bytes 1572872 | tf_op jit(solution)/shard_map/ppermute | solution.py:383
  148.2 0.5 slice.531
  149.3 3.0 %collective-permute-done.6 = f32[4,4,8,1024]{3,2,1,0:T(8,128)S(1)} collective-permute-done((f32[4,4,8,1024]{3,2,1,0:T(8,128)S(1)}, f32[4,4,8,1024]{3,2,1,0:T(8,128)S(1)}, u32[]{:S(2)}, u32[]{:S(2)}) %collective-permute-start.6) | collective-permute-done | bytes 524320 | tf_op jit(solution)/shard_map/ppermute | solution.py:382
  152.4 4.4 %collective-permute-done.7 = f32[4,4,8,1024]{3,2,1,0:T(8,128)S(1)} collective-permute-done((f32[4,4,8,1024]{3,2,1,0:T(8,128)S(1)}, f32[4,4,8,1024]{3,2,1,0:T(8,128)S(1)}, u32[]{:S(2)}, u32[]{:S(2)}) %collective-permute-start.7) | collective-permute-done | bytes 524320 | tf_op jit(solution)/shard_map/ppermute | solution.py:383
  156.8 0.0 copy-done
  156.8 0.0 copy-done.1
  156.8 0.0 copy-done.2
  156.8 0.0 copy-done.3
  156.8 0.0 copy-done.4
  156.8 11.9 %conditional.1 = (f32[8,4,16,1024]{3,2,1,0:T(8,128)}) conditional(s32[]{:T(128)} %bitcast.11, (s32[4,16]{1,0:T(4,128)S(1)}, f32[4,4,8,1024]{3,2,1,0:T(8,128)S(1)}, f32[4,16,8,1024]{3,2,1,0:T(8,128)S(1)}, f32[4,4,8,1024]{3,2,1,0:T(8,128)S(1)}) %tuple.34, (s32[4,16]{1,0:T(4,128)S(1)}, s32[4,16]{1,0:T(4,128)S(1)}, s32[512,1]{0,1:T(1,128)S(1)}, ...), branch_computations={%region_0.0_spmd, %region_1.8_spmd} | conditional | flops 1742528768 | bytes 319463456 | solution.py:473
  156.8 11.9 %branch_0_fun.1 = f32[8,4,16,1024]{3,2,1,0:T(8,128)} custom-call(s32[4,16]{1,0:T(4,128)S(1)} %get-tuple-element.28.dips, f32[4,4,8,1024]{3,2,1,0:T(8,128)S(1)} %get-tuple-element.29.left, f32[4,16,8,1024]{3,2,1,0:T(8,128)S(1)} %get-tuple-element.30.own, f32[4,4,8,1024]{3,2,1,0:T(8,128)S(1)} %get-tuple-element.31.right), custom_call_target="tpu_custom_call" | custom-call | tf_op jit(solution)/shard_map/cond/branch_0_fun/pallas_call | solution.py:360
Async XLA Ops:
  63.5 54.2 %collective-permute-start.4 = (f32[4,16,8,1024]{3,2,1,0:T(8,128)S(1)}, f32[4,16,8,1024]{3,2,1,0:T(8,128)S(1)}, u32[]{:S(2)}, u32[]{:S(2)}) collective-permute-start(f32[4,16,8,1024]{3,2,1,0:T(8,128)S(1)} %bitcast.26), channel_id=1, source_target_pairs={{0,8},{8,16},{16,24},{24,32},{32,40},{40,48},{48,56},{56,64},{64,7... | collective-permute-start | bytes 6291464 | tf_op jit(solution)/shard_map/ppermute | solution.py:382
  73.1 58.1 %collective-permute-start.5 = (f32[4,16,8,1024]{3,2,1,0:T(8,128)S(1)}, f32[4,16,8,1024]{3,2,1,0:T(8,128)S(1)}, u32[]{:S(2)}, u32[]{:S(2)}) collective-permute-start(f32[4,16,8,1024]{3,2,1,0:T(8,128)S(1)} %bitcast.27), channel_id=1, source_target_pairs={{8,0},{16,8},{24,16},{32,24},{40,32},{48,40},{56,48},{64,56},{72,6... | collective-permute-start | bytes 6291464 | tf_op jit(solution)/shard_map/ppermute | solution.py:383
  141.6 15.1 %copy-start = (s32[512,1]{0,1:T(1,128)S(1)}, s32[512,1]{0,1:T(1,128)}, u32[]{:S(2)}) copy-start(s32[512,1]{0,1:T(1,128)} %param.9) | copy-start | bytes 6148
  141.7 15.1 %copy-start.1 = (s32[512]{0:T(512)S(1)}, s32[512]{0:T(512)}, u32[]{:S(2)}) copy-start(s32[512]{0:T(512)} %param.10) | copy-start | bytes 6148
  141.7 15.1 %copy-start.2 = (s32[512]{0:T(512)S(1)}, s32[512]{0:T(512)}, u32[]{:S(2)}) copy-start(s32[512]{0:T(512)} %param.11) | copy-start | bytes 6148
  141.7 15.1 %copy-start.3 = (s32[4,16]{1,0:T(4,128)S(1)}, s32[4,16]{1,0:T(4,128)}, u32[]{:S(2)}) copy-start(s32[4,16]{1,0:T(4,128)} %param.13) | copy-start | bytes 772
  141.7 15.1 %copy-start.4 = (s32[4,16]{1,0:T(4,128)S(1)}, s32[4,16]{1,0:T(4,128)}, u32[]{:S(2)}) copy-start(s32[4,16]{1,0:T(4,128)} %dips.1) | copy-start | bytes 772
  141.8 10.5 %collective-permute-start.6 = (f32[4,4,8,1024]{3,2,1,0:T(8,128)S(1)}, f32[4,4,8,1024]{3,2,1,0:T(8,128)S(1)}, u32[]{:S(2)}, u32[]{:S(2)}) collective-permute-start(f32[4,4,8,1024]{3,2,1,0:T(8,128)S(1)} %get-tuple-element.60), channel_id=1, source_target_pairs={{0,1},{1,2},{2,3},{3,4},{4,5},{5,6},{6,7},{8,9},{9,10},{10,11},{11... | collective-permute-start | bytes 1572872 | tf_op jit(solution)/shard_map/ppermute | solution.py:382
  146.2 10.5 %collective-permute-start.7 = (f32[4,4,8,1024]{3,2,1,0:T(8,128)S(1)}, f32[4,4,8,1024]{3,2,1,0:T(8,128)S(1)}, u32[]{:S(2)}, u32[]{:S(2)}) collective-permute-start(f32[4,4,8,1024]{3,2,1,0:T(8,128)S(1)} %get-tuple-element.59), channel_id=1, source_target_pairs={{1,0},{2,1},{3,2},{4,3},{5,4},{6,5},{7,6},{9,8},{10,9},{11,10},{12... | collective-permute-start | bytes 1572872 | tf_op jit(solution)/shard_map/ppermute | solution.py:383

commit v2 on v1

--- a/solution.py
+++ b/solution.py
@@ -14,6 +14,7 @@
 N_Z = 8
 N_P = 32
 N_XL = 8
+N_IL = 32
 CAP = 6
 POOL = 96
 SLOTS = N_Z * CAP
@@ -33,9 +34,11 @@
 
 
 def route_kernel(
-    traces, dest, bins, offs, stacked, flag_out,
-    rows, p1, send1, recv1, lab1s, lab1r, l2, p2, send2, recv2, lab2s, lab2r, wide, sel, count,
+    traces, dest, bins, offs, ext, flag_out,
+    rows, eye, p1, send1, recv1, lab1s, lab1r, l2, p2, send2, recv2, lab2s, lab2r, wide, sel, count,
+    rim_q, rim_s, got_q, got_s,
     s1_send, s1_recv, l1_send, l1_recv, s2_send, s2_recv, l2_send, l2_recv,
+    q_send, q_recv, f_send, f_recv,
 ):
     n, samples = traces.shape
     w = samples // T
@@ -53,7 +56,12 @@
         p = lax.rem(my_p + k, N_P)
         return p, ((p // N_XL) * N_Z + my_z, lax.rem(p, N_XL))
 
+    def rim_peer(side):
+        return (lax.rem(me_i + (1 if side == 0 else N_IL - 1), N_IL), me_x)
+
     barrier = pltpu.get_barrier_semaphore()
+    for side in range(2):
+        pl.semaphore_signal(barrier, inc=1, device_id=rim_peer(side), device_id_type=MESH)
 
     @pl.loop(1, N_Z)
     def _(k):
@@ -64,9 +72,9 @@
         pl.semaphore_signal(barrier, inc=1, device_id=p_peer(k)[1], device_id_type=MESH)
 
     d = dest[...]
-    eye = onehot(iota((n, n), 0) == iota((n, n), 1))
+    eye[...] = onehot(iota((n, n), 0) == iota((n, n), 1))
     wide_d = jnp.broadcast_to(d.astype(f32), (128, n)).astype(bf16)
-    dcol = lax.dot_general(eye, wide_d, NT, preferred_element_type=f32).astype(i32)
+    dcol = lax.dot_general(eye[...], wide_d, NT, preferred_element_type=f32).astype(i32)
     zcol = (dcol >> 3) & 7
     for t in range(n // 128):
         lanes = slice(t * 128, (t + 1) * 128)
@@ -104,7 +112,7 @@
     def _(i):
         recv1[i // N_Z, lax.rem(i, N_Z), POOL:, :] = jnp.zeros((128 - POOL, w), bf16)
 
-    pl.semaphore_wait(barrier, N_Z - 1 + N_P - 1)
+    pl.semaphore_wait(barrier, N_Z - 1 + N_P - 1 + 2)
 
     def lab1_copy(k):
         z, peer = z_peer(k)
@@ -230,8 +238,49 @@
             row2_copy(t, k).wait()
 
         total = jnp.dot(sel[...], recv2[t].reshape(ROWS, w), preferred_element_type=f32)
+        parts = [total[:, c * 128:(c + 1) * 128] / count[...] for c in range(w // 128)]
+        top = jnp.abs(parts[0])
+        for c, part in enumerate(parts):
+            ext[CELLS:2 * CELLS, t * w + c * 128:t * w + (c + 1) * 128] = part
+            top = jnp.maximum(top, jnp.abs(part))
+        step = (jnp.max(top, axis=1, keepdims=True) * (1.01 / 32767.0)).astype(bf16)
+        step = jnp.broadcast_to(step, (CELLS, 128))
+        size = step.astype(f32)
+        fine = jnp.where(size > 0.0, 1.0 / size, 0.0)
+        for c, part in enumerate(parts):
+            rim_q[t, :, c * 128:(c + 1) * 128] = jnp.round(part * fine).astype(i32).astype(jnp.int16)
+        first_lane = onehot(iota((16, 128), 1) == 0)
+        rim_s[t] = lax.dot_general(first_lane, step, NT, preferred_element_type=f32)[:8]
+        for side in range(2):
+            for copy in rim_copies(t, side):
+                copy.start()
+
+    def rim_copies(t, side):
+        peer = rim_peer(side)
+        return (
+            pltpu.make_async_remote_copy(
+                src_ref=rim_s.at[t], dst_ref=got_s.at[side, t],
+                send_sem=f_send.at[side, t], recv_sem=f_recv.at[side, t],
+                device_id=peer, device_id_type=MESH,
+            ),
+            pltpu.make_async_remote_copy(
+                src_ref=rim_q.at[t], dst_ref=got_q.at[side, t],
+                send_sem=q_send.at[side, t], recv_sem=q_recv.at[side, t],
+                device_id=peer, device_id_type=MESH,
+            ),
+        )
+
+    def rim(t, side):
+        for copy in rim_copies(t, side):
+            copy.wait()
+        row = jnp.broadcast_to(got_s[side, t][0:1, :], (128, CELLS)).astype(bf16)
+        size = lax.dot_general(eye[...], row, NT, preferred_element_type=f32)
+        outside = me_i == (0 if side == 0 else N_IL - 1)
+        size = size * jnp.where(outside, 0.0, 1.0)
+        base = 0 if side == 0 else 2 * CELLS
         for c in range(w // 128):
-            stacked[:, t * w + c * 128:t * w + (c + 1) * 128] = total[:, c * 128:(c + 1) * 128] / count[...]
+            value = got_q[side, t, :, c * 128:(c + 1) * 128].astype(f32)
+            ext[base:base + CELLS, t * w + c * 128:t * w + (c + 1) * 128] = value * size
 
     for t in range(T):
         forward(t)
@@ -240,6 +289,9 @@
         if t > 0:
             stack(t - 1)
     stack(T - 1)
+    for t in range(T):
+        for side in range(2):
+            rim(t, side)
 
 
 def route(traces, dest, bins, offs):
@@ -250,13 +302,14 @@
     return pl.pallas_call(
         route_kernel,
         out_shape=(
-            jax.ShapeDtypeStruct((CELLS, samples), f32),
+            jax.ShapeDtypeStruct((3 * CELLS, samples), f32),
             jax.ShapeDtypeStruct((8, 128), i32),
         ),
         in_specs=[vmem] * 4,
         out_specs=(vmem, vmem),
         scratch_shapes=[
             pltpu.VMEM((8, n), f32),
+            pltpu.VMEM((n, n), bf16),
             pltpu.VMEM((N_Z, 128, n), bf16),
             pltpu.VMEM((T, N_Z, POOL, w), bf16),
             pltpu.VMEM((T, N_Z, 128, w), bf16),
@@ -271,8 +324,13 @@
             pltpu.VMEM((8, ROWS), i32),
             pltpu.VMEM((CELLS, ROWS), bf16),
             pltpu.VMEM((CELLS, 128), f32),
+            pltpu.VMEM((T, CELLS, w), jnp.int16),
+            pltpu.VMEM((T, 8, CELLS), f32),
+            pltpu.VMEM((2, T, CELLS, w), jnp.int16),
+            pltpu.VMEM((2, T, 8, CELLS), f32),
             dma((T, N_Z)), dma((T, N_Z)), dma((N_Z,)), dma((N_Z,)),
             dma((T, N_P)), dma((T, N_P)), dma((N_P,)), dma((N_P,)),
+            dma((2, T)), dma((2, T)), dma((2, T)), dma((2, T)),
         ],
         compiler_params=pltpu.CompilerParams(
             collective_id=0, has_side_effects=True, vmem_limit_bytes=48 * 1024 * 1024
@@ -280,76 +338,85 @@
     )(traces, dest, bins, offs)
 
 
-def steer(blocks, dip):
-    samples = blocks(0).shape[1]
+def steer(at, dip, samples):
     parts = samples // 128
     lane = iota((8, 128), 1)
 
-    def signed(up):
-        acc = [FILTER_TAPS[4] * blocks(0)[:, k * 128:(k + 1) * 128] for k in range(parts)]
-        zero = jnp.zeros((8, 128), f32)
-        for j in (-4, -3, -2, -1, 1, 2, 3, 4):
-            shift = j * dip
-            block = blocks(j)
-            turn = lax.rem(128 - shift, 128)
-            turned = [pltpu.roll(block[:, k * 128:(k + 1) * 128], turn, 1) for k in range(parts)]
-            if up == (j > 0):
-                keep = lane < 128 - shift
-                other = turned[1:] + [zero]
+    def piece(j, k):
+        ref, index = at(j)
+        if isinstance(k, int):
+            return ref[index + (slice(None), slice(k * 128, (k + 1) * 128))]
+        return ref[index + (slice(None), pl.ds(pl.multiple_of(k * 128, 128), 128))]
+
+    def moved(j):
+        shift = j * dip
+        ahead = jnp.where(shift > 0, 1, 0)
+        keep = (lane >= jnp.maximum(shift, 0)) & (lane < 128 + jnp.minimum(shift, 0))
+        turn = lax.rem(128 - shift, 128)
+        out = []
+        for k in range(parts):
+            if k == 0:
+                other = piece(j, 1) * ahead.astype(f32)
+            elif k == parts - 1:
+                other = piece(j, k - 1) * (1 - ahead).astype(f32)
             else:
-                keep = lane >= -shift
-                other = [zero] + turned[:-1]
-            for k in range(parts):
-                acc[k] += FILTER_TAPS[j + 4] * jnp.where(keep, turned[k], other[k])
-        return acc
-
-    return lax.cond(dip >= 0, lambda: signed(True), lambda: signed(False))
-
-
-def inline_kernel(dips, before, own, after, out):
-    n_il, n_xl = own.shape[0], own.shape[1]
+                other = piece(j, k - 1 + 2 * ahead)
+            out.append(pltpu.roll(jnp.where(keep, piece(j, k), other), turn, 1))
+        return out
+
+    acc = [FILTER_TAPS[4] * piece(0, k) for k in range(parts)]
+    for j in (1, 2, 3, 4):
+        up, down = moved(j), moved(-j)
+        for k in range(parts):
+            acc[k] += FILTER_TAPS[4 + j] * (up[k] + down[k])
+    return acc
+
+
+def inline_kernel(dips, ext, out):
+    n_il, n_xl, _, samples = out.shape
     base = pl.program_id(0) * n_xl
 
-    @pl.loop(0, n_xl)
-    def _(x):
+    def column(x, carry):
         for i in range(n_il):
-            def blocks(j, i=i):
-                at = i + j
-                ref = before if at < 0 else own if at < n_il else after
-                return ref[at % n_il, x]
-
-            acc = steer(blocks, dips[i, base + x])
+            acc = steer(lambda j, i=i: (ext, (i + 4 + j, x)), dips[i, base + x], samples)
             for k, part in enumerate(acc):
                 out[i, x, :, k * 128:(k + 1) * 128] = part
-
-
-def inline_pass(dips, before, own, after):
-    n_il, n_xl, _, samples = own.shape
+        return carry
+
+    lax.fori_loop(0, n_xl, column, 0, unroll=2)
+
+
+def inline_pass(dips, ext):
+    n_il, n_xl = dips.shape
+    samples = ext.shape[-1]
     step = 4
-    block = pl.BlockSpec((n_il, step, OFFSETS, samples), lambda s: (0, s, 0, 0))
     return pl.pallas_call(
         inline_kernel,
         grid=(n_xl // step,),
-        out_shape=jax.ShapeDtypeStruct(own.shape, f32),
-        in_specs=[pl.BlockSpec(memory_space=pltpu.SMEM), block, block, block],
-        out_specs=block,
+        out_shape=jax.ShapeDtypeStruct((n_il, n_xl, OFFSETS, samples), f32),
+        in_specs=[
+            pl.BlockSpec(memory_space=pltpu.SMEM),
+            pl.BlockSpec((3 * n_il, step, OFFSETS, samples), lambda s: (0, s, 0, 0)),
+        ],
+        out_specs=pl.BlockSpec((n_il, step, OFFSETS, samples), lambda s: (0, s, 0, 0)),
         compiler_params=pltpu.CompilerParams(vmem_limit_bytes=32 * 1024 * 1024),
-    )(dips, before, own, after)
+    )(dips, ext)
 
 
 def xline_kernel(dips, left, own, right, out, ext, turned):
-    n_xl = own.shape[1]
+    n_xl, samples = own.shape[1], own.shape[3]
     il = pl.program_id(0)
     ext[0:4] = left[0]
     ext[4:4 + n_xl] = own[0]
     ext[4 + n_xl:] = right[0]
 
-    @pl.loop(0, n_xl)
-    def _(x):
-        acc = steer(lambda j: ext[x + 4 + j], dips[il, x])
+    def column(x, carry):
+        acc = steer(lambda j: (ext, (x + 4 + j,)), dips[il, x], samples)
         for k, part in enumerate(acc):
             turned[k, pl.ds(x, OFFSETS, stride=n_xl), :] = part
-
+        return carry
+
+    lax.fori_loop(0, n_xl, column, 0, unroll=8)
     for k in range(turned.shape[0]):
         out[:, 0, :, k * 128:(k + 1) * 128] = turned[k].reshape(OFFSETS, n_xl, 128)
 
@@ -461,12 +528,10 @@
 def per_device(traces, destination, bin_local, offset_class, dip_inline, dip_xline):
     n, samples = traces.shape
     n_il, n_xl = dip_inline.shape
-    stacked, flag = route(
+    ext, flag = route(
         traces, destination.reshape(1, n), bin_local.reshape(1, n), offset_class.reshape(1, n)
     )
-    stacked = stacked.reshape(n_il, n_xl, OFFSETS, samples)
-    up, down = shifted(stacked, "inline")
-    first = inline_pass(dip_inline, up(stacked), stacked, down(stacked))
+    first = inline_pass(dip_inline, ext.reshape(3 * n_il, n_xl, OFFSETS, samples))
     right, left = shifted(first, "xline")
     from_left = right(first[:, n_xl - 4:])
     from_right = left(first[:, :4])

time: 169 us -> 143 us (0.85)
  the two profiles are of different devices: /device:TPU:49 before, /device:TPU:19 now
where the time goes in v2:
time: 143 us
  Pallas kernels  125 us (87%)
  waiting for transfers between devices  7.4 us (5%)
  starting transfers between devices  6.24 us (4%)
  local copies, waits for them, and re-layouts  3.42 us (2%)
    pallas_call x1, Pallas kernels, route(): pl.pallas_call(route_kernel, out_shape=(jax.ShapeDtypeStruct((3 * CELLS,...  106 us
    pallas_call x1, Pallas kernels, xline_pass(): pl.pallas_call(xline_kernel, grid=(n_il,), out_shape=jax.ShapeDtypeStruct...  10.2 us
    pallas_call x1, Pallas kernels, inline_pass(): pl.pallas_call(inline_kernel, grid=(n_xl // step,), out_shape=jax.ShapeDt...  8.86 us
    ppermute x1, waiting for transfers between devices, shifted(): lax.ppermute(head, axis, [(i + 1, i) for i in range(count - 1)])  4.4 us
    ppermute x1, starting transfers between devices, shifted(): lax.ppermute(tail, axis, [(i, i + 1) for i in range(count - 1)])  4.31 us
    ppermute x1, waiting for transfers between devices, shifted(): lax.ppermute(tail, axis, [(i, i + 1) for i in range(count - 1)])  3.01 us
  transfers between devices with their start and end apart: 2, of which 2 were waited for; matrix products, arithmetic and copies ran while one was open for 0% of the time, Pallas kernels for 0%

profile of v2, /device:TPU:19, one launch (start us, length us, event | category | flops | bytes accessed | tf_op | source)
XLA Modules:
  0.0 143.2 jit_solution(17639394483446105247)
XLA Ops:
  0.0 106.2 %shard_map.66 = (f32[1536,1024]{1,0:T(8,128)}, s32[8,128]{1,0:T(8,128)S(1)}) custom-call(bf16[512,1024]{1,0:T(8,128)(2,1)} %traces.1, s32[1,512]{1,0:T(1,128)} %bitcast.35, s32[1,512]{1,0:T(1,128)} %bitcast.39, s32[1,512]{1,0:T(1,128)} %bitcast.40), custom_call_target="tpu_custom_call" | custom-call | tf_op jit(solution)/shard_map/pallas_call | solution.py:302
  106.2 0.0 copy-start
  106.2 2.8 %copy-done = f32[1536,1024]{1,0:T(8,128)S(1)} copy-done((f32[1536,1024]{1,0:T(8,128)S(1)}, f32[1536,1024]{1,0:T(8,128)}, u32[]{:S(2)}) %copy-start) | copy-done | bytes 6291480
  109.0 8.9 %shard_map.67 = f32[4,16,8,1024]{3,2,1,0:T(8,128)S(1)} custom-call(s32[4,16]{1,0:T(4,128)} %dips.1, f32[12,16,8,1024]{3,2,1,0:T(8,128)S(1)} %bitcast.26), custom_call_target="tpu_custom_call" | custom-call | tf_op jit(solution)/shard_map/pallas_call | solution.py:393
  117.9 0.0 copy-start.1
  117.9 0.0 copy-start.2
  117.9 0.0 copy-start.3
  117.9 0.0 copy-start.4
  117.9 0.0 copy-start.5
  118.0 0.1 fusion.155
  118.1 4.3 %collective-permute-start.4 = (f32[4,4,8,1024]{3,2,1,0:T(8,128)S(1)}, f32[4,4,8,1024]{3,2,1,0:T(8,128)S(1)}, u32[]{:S(2)}, u32[]{:S(2)}) collective-permute-start(f32[4,4,8,1024]{3,2,1,0:T(8,128)S(1)} %get-tuple-element.60), channel_id=1, source_target_pairs={{0,1},{1,2},{2,3},{3,4},{4,5},{5,6},{6,7},{8,9},{9,10},{10,11},{11... | collective-permute-start | bytes 1572872 | tf_op jit(solution)/shard_map/ppermute | solution.py:449
  122.4 1.9 %collective-permute-start.5 = (f32[4,4,8,1024]{3,2,1,0:T(8,128)S(1)}, f32[4,4,8,1024]{3,2,1,0:T(8,128)S(1)}, u32[]{:S(2)}, u32[]{:S(2)}) collective-permute-start(f32[4,4,8,1024]{3,2,1,0:T(8,128)S(1)} %get-tuple-element.59), channel_id=1, source_target_pairs={{1,0},{2,1},{3,2},{4,3},{5,4},{6,5},{7,6},{9,8},{10,9},{11,10},{12... | collective-permute-start | bytes 1572872 | tf_op jit(solution)/shard_map/ppermute | solution.py:450
  124.3 0.5 slice.531
  125.5 3.0 %collective-permute-done.4 = f32[4,4,8,1024]{3,2,1,0:T(8,128)S(1)} collective-permute-done((f32[4,4,8,1024]{3,2,1,0:T(8,128)S(1)}, f32[4,4,8,1024]{3,2,1,0:T(8,128)S(1)}, u32[]{:S(2)}, u32[]{:S(2)}) %collective-permute-start.4) | collective-permute-done | bytes 524320 | tf_op jit(solution)/shard_map/ppermute | solution.py:449
  128.5 4.4 %collective-permute-done.5 = f32[4,4,8,1024]{3,2,1,0:T(8,128)S(1)} collective-permute-done((f32[4,4,8,1024]{3,2,1,0:T(8,128)S(1)}, f32[4,4,8,1024]{3,2,1,0:T(8,128)S(1)}, u32[]{:S(2)}, u32[]{:S(2)}) %collective-permute-start.5) | collective-permute-done | bytes 524320 | tf_op jit(solution)/shard_map/ppermute | solution.py:450
  132.9 0.0 copy-done.1
  132.9 0.0 copy-done.2
  132.9 0.0 copy-done.3
  132.9 0.0 copy-done.4
  132.9 0.0 copy-done.5
  132.9 10.2 %conditional.1 = (f32[8,4,16,1024]{3,2,1,0:T(8,128)}) conditional(s32[]{:T(128)} %bitcast.11, (s32[4,16]{1,0:T(4,128)S(1)}, f32[4,4,8,1024]{3,2,1,0:T(8,128)S(1)}, f32[4,16,8,1024]{3,2,1,0:T(8,128)S(1)}, f32[4,4,8,1024]{3,2,1,0:T(8,128)S(1)}) %tuple.34, (s32[4,16]{1,0:T(4,128)S(1)}, s32[4,16]{1,0:T(4,128)S(1)}, s32[512,1]{0,1:T(1,128)S(1)}, ...), branch_computations={%region_0.0_spmd, %region_1.8_spmd} | conditional | flops 1742528768 | bytes 319463456 | solution.py:538
  132.9 10.2 %branch_0_fun.1 = f32[8,4,16,1024]{3,2,1,0:T(8,128)} custom-call(s32[4,16]{1,0:T(4,128)S(1)} %get-tuple-element.28.dips, f32[4,4,8,1024]{3,2,1,0:T(8,128)S(1)} %get-tuple-element.29.left, f32[4,16,8,1024]{3,2,1,0:T(8,128)S(1)} %get-tuple-element.30.own, f32[4,4,8,1024]{3,2,1,0:T(8,128)S(1)} %get-tuple-element.31.right), custom_call_target="tpu_custom_call" | custom-call | tf_op jit(solution)/shard_map/cond/branch_0_fun/pallas_call | solution.py:427
Async XLA Ops:
  106.2 2.8 %copy-start = (f32[1536,1024]{1,0:T(8,128)S(1)}, f32[1536,1024]{1,0:T(8,128)}, u32[]{:S(2)}) copy-start(f32[1536,1024]{1,0:T(8,128)} %get-tuple-element.41) | copy-start | bytes 18874372
  117.9 15.0 %copy-start.1 = (s32[512,1]{0,1:T(1,128)S(1)}, s32[512,1]{0,1:T(1,128)}, u32[]{:S(2)}) copy-start(s32[512,1]{0,1:T(1,128)} %param.9) | copy-start | bytes 6148
  117.9 15.0 %copy-start.2 = (s32[512]{0:T(512)S(1)}, s32[512]{0:T(512)}, u32[]{:S(2)}) copy-start(s32[512]{0:T(512)} %param.10) | copy-start | bytes 6148
  117.9 15.0 %copy-start.3 = (s32[512]{0:T(512)S(1)}, s32[512]{0:T(512)}, u32[]{:S(2)}) copy-start(s32[512]{0:T(512)} %param.11) | copy-start | bytes 6148
  117.9 15.0 %copy-start.4 = (s32[4,16]{1,0:T(4,128)S(1)}, s32[4,16]{1,0:T(4,128)}, u32[]{:S(2)}) copy-start(s32[4,16]{1,0:T(4,128)} %param.13) | copy-start | bytes 772
  117.9 15.0 %copy-start.5 = (s32[4,16]{1,0:T(4,128)S(1)}, s32[4,16]{1,0:T(4,128)}, u32[]{:S(2)}) copy-start(s32[4,16]{1,0:T(4,128)} %dips.1) | copy-start | bytes 772
  118.1 10.4 %collective-permute-start.4 = (f32[4,4,8,1024]{3,2,1,0:T(8,128)S(1)}, f32[4,4,8,1024]{3,2,1,0:T(8,128)S(1)}, u32[]{:S(2)}, u32[]{:S(2)}) collective-permute-start(f32[4,4,8,1024]{3,2,1,0:T(8,128)S(1)} %get-tuple-element.60), channel_id=1, source_target_pairs={{0,1},{1,2},{2,3},{3,4},{4,5},{5,6},{6,7},{8,9},{9,10},{10,11},{11... | collective-permute-start | bytes 1572872 | tf_op jit(solution)/shard_map/ppermute | solution.py:449
  122.4 10.5 %collective-permute-start.5 = (f32[4,4,8,1024]{3,2,1,0:T(8,128)S(1)}, f32[4,4,8,1024]{3,2,1,0:T(8,128)S(1)}, u32[]{:S(2)}, u32[]{:S(2)}) collective-permute-start(f32[4,4,8,1024]{3,2,1,0:T(8,128)S(1)} %get-tuple-element.59), channel_id=1, source_target_pairs={{1,0},{2,1},{3,2},{4,3},{5,4},{6,5},{7,6},{9,8},{10,9},{11,10},{12... | collective-permute-start | bytes 1572872 | tf_op jit(solution)/shard_map/ppermute | solution.py:450

commit v3 on v2

--- a/solution.py
+++ b/solution.py
@@ -20,6 +20,7 @@
 SLOTS = N_Z * CAP
 ROWS = N_P * SLOTS
 CELLS = 512
+BINS = CELLS // OFFSETS
 T = 4
 NT = (((1,), (1,)), ((), ()))
 f32, bf16, i32 = jnp.float32, jnp.bfloat16, jnp.int32
@@ -33,12 +34,40 @@
     return jnp.where(mask, 1.0, 0.0).astype(bf16)
 
 
+def steer(at, dip, parts, ks):
+    lane = iota((OFFSETS, 128), 1)
+    zero = jnp.zeros((OFFSETS, 128), f32)
+
+    def piece(j, k):
+        if not 0 <= k < parts:
+            return zero
+        ref, index = at(j)
+        return ref[index + (slice(None), slice(k * 128, (k + 1) * 128))]
+
+    def moved(j):
+        shift = j * dip
+        after = lane < shift
+        before = lane >= 128 + shift
+        turn = lax.rem(128 - shift, 128)
+        row = [piece(j, k) for k in range(ks[0] - 1, ks[-1] + 2)]
+        return [
+            pltpu.roll(jnp.where(after, row[i + 2], jnp.where(before, row[i], row[i + 1])), turn, 1)
+            for i in range(len(ks))
+        ]
+
+    acc = [FILTER_TAPS[4] * piece(0, k) for k in ks]
+    for j in (1, 2, 3, 4):
+        up, down = moved(j), moved(-j)
+        acc = [a + FILTER_TAPS[4 + j] * (u + v) for a, u, v in zip(acc, up, down)]
+    return acc
+
+
 def route_kernel(
-    traces, dest, bins, offs, ext, flag_out,
-    rows, eye, p1, send1, recv1, lab1s, lab1r, l2, p2, send2, recv2, lab2s, lab2r, wide, sel, count,
-    rim_q, rim_s, got_q, got_s,
+    dips, traces, dest, bins, offs, out, flag_out,
+    ext, rows, eye, p1, send1, recv1, lab1s, lab1r, l2, p2, send2, recv2, lab2s, lab2r, wide, sel, count,
+    rim_q, rim_s, got_q, got_s, edge, got_e,
     s1_send, s1_recv, l1_send, l1_recv, s2_send, s2_recv, l2_send, l2_recv,
-    q_send, q_recv, f_send, f_recv,
+    q_send, q_recv, f_send, f_recv, e_send, e_recv,
 ):
     n, samples = traces.shape
     w = samples // T
@@ -101,16 +130,12 @@
     def _(z):
         target = jnp.where(zrow == z, place, -1)
         pick = onehot(iota((128, n), 0) == target)
-        p1[z] = pick
+        p1[z] = pick[:POOL]
         lab = lax.dot_general(labels, pick, NT, preferred_element_type=f32)[:8].astype(i32)
         lab = jnp.where(iota((8, 128), 1) < POOL, lab, 0)
         lab1s[z] = jnp.where(iota((8, 128), 0) == 4, over, lab)
 
     lab1r[my_z] = lab1s[my_z]
-
-    @pl.loop(0, T * N_Z)
-    def _(i):
-        recv1[i // N_Z, lax.rem(i, N_Z), POOL:, :] = jnp.zeros((128 - POOL, w), bf16)
 
     pl.semaphore_wait(barrier, N_Z - 1 + N_P - 1 + 2)
 
@@ -125,7 +150,7 @@
     def row1_copy(t, k):
         z, peer = z_peer(k)
         return pltpu.make_async_remote_copy(
-            src_ref=send1.at[t, z], dst_ref=recv1.at[t, my_z, pl.ds(0, POOL), :],
+            src_ref=send1.at[t, z], dst_ref=recv1.at[t, my_z],
             send_sem=s1_send.at[t, k], recv_sem=s1_recv.at[t, k],
             device_id=peer, device_id_type=MESH,
         )
@@ -150,37 +175,39 @@
     def _(k):
         lab1_copy(k).start()
 
-    for t in range(T):
-        cols = slice(t * w, (t + 1) * w)
-
-        def picked(z, cols=cols):
-            return jnp.dot(p1[z][:POOL], traces[:, cols], preferred_element_type=f32).astype(bf16)
+    def send_rows(t):
+        picked = jnp.dot(
+            p1[...].reshape(N_Z * POOL, n), traces[:, t * w:(t + 1) * w], preferred_element_type=f32
+        )
+        send1[t] = picked.astype(bf16).reshape(N_Z, POOL, w)
 
         @pl.loop(1, N_Z)
-        def _(k, t=t, picked=picked):
-            z, _peer = z_peer(k)
-            send1[t, z] = picked(z)
+        def _(k):
             row1_copy(t, k).start()
 
-        recv1[t, my_z, 0:POOL, :] = picked(my_z)
+        recv1[t, my_z] = send1[t, my_z]
+
+    send_rows(0)
+    send_rows(1)
 
     @pl.loop(1, N_Z)
     def _(k):
         lab1_copy(k).wait()
 
-    def seen(z, worst):
-        lab = lab1r[z]
-        code = lab[1:2, :]
-        target = jnp.where(code > 0, lab[0:1, :] * SLOTS + code - 1, -1)
-        lanes = pl.ds(pl.multiple_of(z * 128, 128), 128)
-        p2[:, lanes] = onehot(iota((ROWS, 128), 0) == target)
-        l2[:, lanes] = jnp.concatenate([lab, lab], axis=0).astype(f32).astype(bf16)
-        return jnp.maximum(worst, lab[4:5, :])
-
-    worst = lax.fori_loop(0, N_Z, seen, jnp.zeros((1, 128), i32))
+    lab = jnp.concatenate([lab1r[z][:, :POOL] for z in range(N_Z)], axis=1)
+    code = lab[1:2, :]
+    wide[:, 0:N_Z * POOL] = jnp.where(code > 0, lab[0:1, :] * SLOTS + code - 1, -1) + jnp.zeros_like(lab)
+    l2[...] = jnp.concatenate([lab, lab], axis=0).astype(f32).astype(bf16)
+    worst = jnp.max(lab[4:5, :], axis=1, keepdims=True)
+
+    @pl.loop(0, N_Z * POOL // 128)
+    def _(c):
+        lanes = pl.ds(pl.multiple_of(c * 128, 128), 128)
+        p2[:, lanes] = onehot(iota((ROWS, 128), 0) == wide[0:1, lanes])
+
     lab = lax.dot_general(l2[...], p2[...], NT, preferred_element_type=f32).astype(i32)
     cell = jnp.where(lab[1:2, :] > 0, lab[2:3, :] * OFFSETS + lab[3:4, :], -1)
-    wide[...] = jnp.where(iota((8, ROWS), 0) == 1, worst[:, 0:1], cell)
+    wide[...] = jnp.where(iota((8, ROWS), 0) == 1, worst, cell)
 
     @pl.loop(0, N_P // 8)
     def _(g):
@@ -199,13 +226,13 @@
         def _(k):
             row1_copy(t, k).wait()
 
-        arrived = recv1[t].reshape(N_Z * 128, w)
-
-        @pl.loop(0, N_P // 8)
-        def _(g):
-            pick = p2[pl.ds(pl.multiple_of(g * 8 * SLOTS, 128), 8 * SLOTS), :]
-            out = jnp.dot(pick, arrived, preferred_element_type=f32).astype(bf16)
-            send2[t, pl.ds(g * 8, 8)] = out.reshape(8, SLOTS, w)
+        if t + 2 < T:
+            send_rows(t + 2)
+        arrived = recv1[t].reshape(N_Z * POOL, w)
+        half = ROWS // 2
+        for g in range(2):
+            moved = jnp.dot(p2[g * half:(g + 1) * half, :], arrived, preferred_element_type=f32)
+            send2[t, g * (N_P // 2):(g + 1) * (N_P // 2)] = moved.astype(bf16).reshape(N_P // 2, SLOTS, w)
 
         @pl.loop(1, N_P)
         def _(k):
@@ -241,7 +268,8 @@
         parts = [total[:, c * 128:(c + 1) * 128] / count[...] for c in range(w // 128)]
         top = jnp.abs(parts[0])
         for c, part in enumerate(parts):
-            ext[CELLS:2 * CELLS, t * w + c * 128:t * w + (c + 1) * 128] = part
+            lanes = slice(t * w + c * 128, t * w + (c + 1) * 128)
+            ext[BINS:2 * BINS, :, lanes] = part.reshape(BINS, OFFSETS, 128)
             top = jnp.maximum(top, jnp.abs(part))
         step = (jnp.max(top, axis=1, keepdims=True) * (1.01 / 32767.0)).astype(bf16)
         step = jnp.broadcast_to(step, (CELLS, 128))
@@ -277,46 +305,96 @@
         size = lax.dot_general(eye[...], row, NT, preferred_element_type=f32)
         outside = me_i == (0 if side == 0 else N_IL - 1)
         size = size * jnp.where(outside, 0.0, 1.0)
-        base = 0 if side == 0 else 2 * CELLS
+        base = 0 if side == 0 else 2 * BINS
         for c in range(w // 128):
             value = got_q[side, t, :, c * 128:(c + 1) * 128].astype(f32)
-            ext[base:base + CELLS, t * w + c * 128:t * w + (c + 1) * 128] = value * size
-
-    for t in range(T):
-        forward(t)
+            lanes = slice(t * w + c * 128, t * w + (c + 1) * 128)
+            ext[base:base + BINS, :, lanes] = (value * size).reshape(BINS, OFFSETS, 128)
+
+    n_il, n_xl = dips.shape
+
+    def edge_copy(t, side):
+        x = lax.rem(me_x + (1 if side == 0 else N_XL - 1), N_XL)
+        return pltpu.make_async_remote_copy(
+            src_ref=edge.at[side, t], dst_ref=got_e.at[side, t],
+            send_sem=e_send.at[side, t], recv_sem=e_recv.at[side, t],
+            device_id=(me_i, x), device_id_type=MESH,
+        )
+
+    def inline_pass(t):
+        ks = range(t * w // 128, (t + 1) * w // 128)
+
+        def column(x):
+            for i in range(n_il):
+                acc = steer(lambda j, i=i: (ext, ((i + 4 + j) * n_xl + x,)), dips[i, x], samples // 128, ks)
+                for k, part in zip(ks, acc):
+                    out[i, x + 4, :, k * 128:(k + 1) * 128] = part
+
+        pl.loop(0, 4)(column)
+        pl.loop(n_xl - 4, n_xl)(column)
+        lanes = slice(t * w, (t + 1) * w)
+        edge[0, t] = out[:, n_xl:n_xl + 4, :, lanes]
+        edge[1, t] = out[:, 4:8, :, lanes]
+        for side in range(2):
+            edge_copy(t, side).start()
+        pl.loop(4, n_xl - 4)(column)
+
+    def edges(t):
+        lanes = slice(t * w, (t + 1) * w)
+        for side in range(2):
+            edge_copy(t, side).wait()
+            outside = me_x == (0 if side == 0 else N_XL - 1)
+            value = got_e[side, t] * jnp.where(outside, 0.0, 1.0)
+            if side == 0:
+                out[:, 0:4, :, lanes] = value
+            else:
+                out[:, n_xl + 4:, :, lanes] = value
+
+    def rims(t):
+        for side in range(2):
+            rim(t, side)
+
+    for t in range(T + 3):
+        if t < T:
+            forward(t)
         if t == 0:
             selector()
-        if t > 0:
+        if 0 <= t - 1 < T:
             stack(t - 1)
-    stack(T - 1)
+        if 0 <= t - 2 < T:
+            rims(t - 2)
+        if 0 <= t - 3 < T - 1:
+            inline_pass(t - 3)
+    inline_pass(T - 1)
     for t in range(T):
-        for side in range(2):
-            rim(t, side)
-
-
-def route(traces, dest, bins, offs):
+        edges(t)
+
+
+def route(dips, traces, dest, bins, offs):
     n, samples = traces.shape
+    n_il, n_xl = dips.shape
     w = samples // T
     vmem = pl.BlockSpec(memory_space=pltpu.VMEM)
     dma = pltpu.SemaphoreType.DMA
     return pl.pallas_call(
         route_kernel,
         out_shape=(
-            jax.ShapeDtypeStruct((3 * CELLS, samples), f32),
+            jax.ShapeDtypeStruct((n_il, n_xl + 8, OFFSETS, samples), f32),
             jax.ShapeDtypeStruct((8, 128), i32),
         ),
-        in_specs=[vmem] * 4,
+        in_specs=[pl.BlockSpec(memory_space=pltpu.SMEM)] + [vmem] * 4,
         out_specs=(vmem, vmem),
         scratch_shapes=[
+            pltpu.VMEM((3 * BINS, OFFSETS, samples), f32),
             pltpu.VMEM((8, n), f32),
             pltpu.VMEM((n, n), bf16),
-            pltpu.VMEM((N_Z, 128, n), bf16),
+            pltpu.VMEM((N_Z, POOL, n), bf16),
             pltpu.VMEM((T, N_Z, POOL, w), bf16),
-            pltpu.VMEM((T, N_Z, 128, w), bf16),
+            pltpu.VMEM((T, N_Z, POOL, w), bf16),
             pltpu.VMEM((N_Z, 8, 128), i32),
             pltpu.VMEM((N_Z, 8, 128), i32),
-            pltpu.VMEM((16, N_Z * 128), bf16),
-            pltpu.VMEM((ROWS, N_Z * 128), bf16),
+            pltpu.VMEM((16, N_Z * POOL), bf16),
+            pltpu.VMEM((ROWS, N_Z * POOL), bf16),
             pltpu.VMEM((T, N_P, SLOTS, w), bf16),
             pltpu.VMEM((T, N_P, SLOTS, w), bf16),
             pltpu.VMEM((N_P, 8, 128), i32),
@@ -328,127 +406,49 @@
             pltpu.VMEM((T, 8, CELLS), f32),
             pltpu.VMEM((2, T, CELLS, w), jnp.int16),
             pltpu.VMEM((2, T, 8, CELLS), f32),
+            pltpu.VMEM((2, T, n_il, 4, OFFSETS, w), f32),
+            pltpu.VMEM((2, T, n_il, 4, OFFSETS, w), f32),
             dma((T, N_Z)), dma((T, N_Z)), dma((N_Z,)), dma((N_Z,)),
             dma((T, N_P)), dma((T, N_P)), dma((N_P,)), dma((N_P,)),
-            dma((2, T)), dma((2, T)), dma((2, T)), dma((2, T)),
+            dma((2, T)), dma((2, T)), dma((2, T)), dma((2, T)), dma((2, T)), dma((2, T)),
         ],
         compiler_params=pltpu.CompilerParams(
             collective_id=0, has_side_effects=True, vmem_limit_bytes=48 * 1024 * 1024
         ),
-    )(traces, dest, bins, offs)
-
-
-def steer(at, dip, samples):
-    parts = samples // 128
-    lane = iota((8, 128), 1)
-
-    def piece(j, k):
-        ref, index = at(j)
-        if isinstance(k, int):
-            return ref[index + (slice(None), slice(k * 128, (k + 1) * 128))]
-        return ref[index + (slice(None), pl.ds(pl.multiple_of(k * 128, 128), 128))]
-
-    def moved(j):
-        shift = j * dip
-        ahead = jnp.where(shift > 0, 1, 0)
-        keep = (lane >= jnp.maximum(shift, 0)) & (lane < 128 + jnp.minimum(shift, 0))
-        turn = lax.rem(128 - shift, 128)
-        out = []
-        for k in range(parts):
-            if k == 0:
-                other = piece(j, 1) * ahead.astype(f32)
-            elif k == parts - 1:
-                other = piece(j, k - 1) * (1 - ahead).astype(f32)
-            else:
-                other = piece(j, k - 1 + 2 * ahead)
-            out.append(pltpu.roll(jnp.where(keep, piece(j, k), other), turn, 1))
-        return out
-
-    acc = [FILTER_TAPS[4] * piece(0, k) for k in range(parts)]
-    for j in (1, 2, 3, 4):
-        up, down = moved(j), moved(-j)
-        for k in range(parts):
-            acc[k] += FILTER_TAPS[4 + j] * (up[k] + down[k])
-    return acc
-
-
-def inline_kernel(dips, ext, out):
-    n_il, n_xl, _, samples = out.shape
-    base = pl.program_id(0) * n_xl
+    )(dips, traces, dest, bins, offs)
+
+
+def xline_kernel(dips, ext, out, turned):
+    n_xl, samples = out.shape[2], out.shape[3]
+    il = pl.program_id(0)
+    ks = range(samples // 128)
 
     def column(x, carry):
-        for i in range(n_il):
-            acc = steer(lambda j, i=i: (ext, (i + 4 + j, x)), dips[i, base + x], samples)
-            for k, part in enumerate(acc):
-                out[i, x, :, k * 128:(k + 1) * 128] = part
+        acc = steer(lambda j: (ext, (0, x + 4 + j)), dips[il, x], len(ks), ks)
+        for k, part in zip(ks, acc):
+            turned[k, pl.ds(x, OFFSETS, stride=n_xl), :] = part
         return carry
 
-    lax.fori_loop(0, n_xl, column, 0, unroll=2)
-
-
-def inline_pass(dips, ext):
+    lax.fori_loop(0, n_xl, column, 0, unroll=8)
+    for k in ks:
+        out[:, 0, :, k * 128:(k + 1) * 128] = turned[k].reshape(OFFSETS, n_xl, 128)
+
+
+def xline_pass(dips, ext):
     n_il, n_xl = dips.shape
     samples = ext.shape[-1]
-    step = 4
-    return pl.pallas_call(
-        inline_kernel,
-        grid=(n_xl // step,),
-        out_shape=jax.ShapeDtypeStruct((n_il, n_xl, OFFSETS, samples), f32),
-        in_specs=[
-            pl.BlockSpec(memory_space=pltpu.SMEM),
-            pl.BlockSpec((3 * n_il, step, OFFSETS, samples), lambda s: (0, s, 0, 0)),
-        ],
-        out_specs=pl.BlockSpec((n_il, step, OFFSETS, samples), lambda s: (0, s, 0, 0)),
-        compiler_params=pltpu.CompilerParams(vmem_limit_bytes=32 * 1024 * 1024),
-    )(dips, ext)
-
-
-def xline_kernel(dips, left, own, right, out, ext, turned):
-    n_xl, samples = own.shape[1], own.shape[3]
-    il = pl.program_id(0)
-    ext[0:4] = left[0]
-    ext[4:4 + n_xl] = own[0]
-    ext[4 + n_xl:] = right[0]
-
-    def column(x, carry):
-        acc = steer(lambda j: (ext, (x + 4 + j,)), dips[il, x], samples)
-        for k, part in enumerate(acc):
-            turned[k, pl.ds(x, OFFSETS, stride=n_xl), :] = part
-        return carry
-
-    lax.fori_loop(0, n_xl, column, 0, unroll=8)
-    for k in range(turned.shape[0]):
-        out[:, 0, :, k * 128:(k + 1) * 128] = turned[k].reshape(OFFSETS, n_xl, 128)
-
-
-def xline_pass(dips, left, own, right):
-    n_il, n_xl, _, samples = own.shape
-    side = pl.BlockSpec((1, 4, OFFSETS, samples), lambda s: (s, 0, 0, 0))
     return pl.pallas_call(
         xline_kernel,
         grid=(n_il,),
         out_shape=jax.ShapeDtypeStruct((OFFSETS, n_il, n_xl, samples), f32),
         in_specs=[
             pl.BlockSpec(memory_space=pltpu.SMEM),
-            side,
-            pl.BlockSpec((1, n_xl, OFFSETS, samples), lambda s: (s, 0, 0, 0)),
-            side,
+            pl.BlockSpec((1, n_xl + 8, OFFSETS, samples), lambda s: (s, 0, 0, 0)),
         ],
         out_specs=pl.BlockSpec((OFFSETS, 1, n_xl, samples), lambda s: (0, s, 0, 0)),
-        scratch_shapes=[
-            pltpu.VMEM((n_xl + 8, OFFSETS, samples), f32),
-            pltpu.VMEM((samples // 128, OFFSETS * n_xl, 128), f32),
-        ],
-        compiler_params=pltpu.CompilerParams(vmem_limit_bytes=32 * 1024 * 1024),
-    )(dips, left, own, right)
-
-
-def shifted(cells, axis):
-    count = lax.axis_size(axis)
-    return (
-        lambda tail: lax.ppermute(tail, axis, [(i, i + 1) for i in range(count - 1)]),
-        lambda head: lax.ppermute(head, axis, [(i + 1, i) for i in range(count - 1)]),
-    )
+        scratch_shapes=[pltpu.VMEM((samples // 128, OFFSETS * n_xl, 128), f32)],
+        compiler_params=pltpu.CompilerParams(vmem_limit_bytes=60 * 1024 * 1024),
+    )(dips, ext)
 
 
 def padded_2(cells, sides, width):
@@ -526,19 +526,18 @@
 
 
 def per_device(traces, destination, bin_local, offset_class, dip_inline, dip_xline):
-    n, samples = traces.shape
-    n_il, n_xl = dip_inline.shape
-    ext, flag = route(
-        traces, destination.reshape(1, n), bin_local.reshape(1, n), offset_class.reshape(1, n)
+    n = traces.shape[0]
+    first, flag = route(
+        dip_inline,
+        traces,
+        destination.reshape(1, n),
+        bin_local.reshape(1, n),
+        offset_class.reshape(1, n),
     )
-    first = inline_pass(dip_inline, ext.reshape(3 * n_il, n_xl, OFFSETS, samples))
-    right, left = shifted(first, "xline")
-    from_left = right(first[:, n_xl - 4:])
-    from_right = left(first[:, :4])
     return lax.cond(
         flag[0, 0] > 0,
         lambda: any_load(traces, destination, bin_local, offset_class, dip_inline, dip_xline),
-        lambda: xline_pass(dip_xline, from_left, first, from_right),
+        lambda: xline_pass(dip_xline, first),
     )
 
 

time: 143 us -> 114 us (0.80)
  the two profiles are of different devices: /device:TPU:19 before, /device:TPU:2 now
where the time goes in v3:
time: 114 us
  Pallas kernels  113 us (99%)
    pallas_call x1, Pallas kernels, route(): pl.pallas_call(route_kernel, out_shape=(jax.ShapeDtypeStruct((n_il, n_xl...  106 us
    pallas_call x1, Pallas kernels, xline_pass(): pl.pallas_call(xline_kernel, grid=(n_il,), out_shape=jax.ShapeDtypeStruct...  7.18 us

profile of v3, /device:TPU:2, one launch (start us, length us, event | category | flops | bytes accessed | tf_op | source)
XLA Modules:
  0.0 114.2 jit_solution(5065938140890974765)
XLA Ops:
  0.0 105.7 %shard_map.66 = (f32[4,24,8,1024]{3,2,1,0:T(8,128)S(1)}, s32[8,128]{1,0:T(8,128)S(1)}) custom-call(s32[4,16]{1,0:T(4,128)} %dips.1, bf16[512,1024]{1,0:T(8,128)(2,1)} %traces.1, s32[1,512]{1,0:T(1,128)} %bitcast.33, s32[1,512]{1,0:T(1,128)} %bitcast.37, s32[1,512]{1,0:T(1,128)} %bitcast.38), custom_call_target="tpu_custom_call" | custom-call | tf_op jit(solution)/shard_map/pallas_call | solution.py:379
  105.7 0.5 slice.525
  106.8 7.4 %conditional.1 = (f32[8,4,16,1024]{3,2,1,0:T(8,128)}) conditional(s32[]{:T(128)} %bitcast.11, (s32[4,16]{1,0:T(4,128)}, f32[4,24,8,1024]{3,2,1,0:T(8,128)S(1)}) %tuple.11, (s32[4,16]{1,0:T(4,128)}, s32[4,16]{1,0:T(4,128)}, s32[512,1]{0,1:T(1,128)}, s32[512]{0:T(512)}, s32[512]{0:T(512)}, /*index=5*/bf16[512,1024]{1,0:T(8,128)(2,1)}) %tuple.12), branch_computations={%region_0.0_spmd, %region_1.8_spmd} | conditional | flops 1742528768 | bytes 319490240 | solution.py:537
  107.0 7.2 %branch_0_fun.1 = f32[8,4,16,1024]{3,2,1,0:T(8,128)} custom-call(s32[4,16]{1,0:T(4,128)} %get-tuple-element.24.dips, f32[4,24,8,1024]{3,2,1,0:T(8,128)S(1)} %get-tuple-element.25.ext), custom_call_target="tpu_custom_call" | custom-call | tf_op jit(solution)/shard_map/cond/branch_0_fun/pallas_call | solution.py:440

commit v4 on v3

--- a/solution.py
+++ b/solution.py
@@ -21,7 +21,11 @@
 ROWS = N_P * SLOTS
 CELLS = 512
 BINS = CELLS // OFFSETS
-T = 4
+WIDTHS = (128, 256, 256, 256, 128)
+STARTS = (0, 128, 384, 640, 896)
+T = len(WIDTHS)
+W = max(WIDTHS)
+UNROLL = 4
 NT = (((1,), (1,)), ((), ()))
 f32, bf16, i32 = jnp.float32, jnp.bfloat16, jnp.int32
 
@@ -63,19 +67,38 @@
 
 
 def route_kernel(
-    dips, traces, dest, bins, offs, out, flag_out,
-    ext, rows, eye, p1, send1, recv1, lab1s, lab1r, l2, p2, send2, recv2, lab2s, lab2r, wide, sel, count,
-    rim_q, rim_s, got_q, got_s, edge, got_e,
+    dips, traces_hbm, dest, bins, offs, out_hbm, flag_out,
+    traces, out, ext, rows, eye, p1, send1, recv1, lab1s, lab1r, l2, p2, send2, recv2, lab2s, lab2r, wide, sel, share,
+    rim_q, rim_s, got_q, got_s, relay, edge, got_e,
     s1_send, s1_recv, l1_send, l1_recv, s2_send, s2_recv, l2_send, l2_recv,
-    q_send, q_recv, f_send, f_recv, e_send, e_recv,
+    q_send, q_recv, f_send, f_recv, e_send, e_recv, r_send, r_recv, in_sem, out_sem,
 ):
     n, samples = traces.shape
-    w = samples // T
+    parts = samples // 128
+
+    def span(t):
+        return slice(STARTS[t], STARTS[t] + WIDTHS[t])
+
+    def wide_of(t):
+        return pl.ds(0, WIDTHS[t])
+
     me_i = lax.axis_index("inline")
     me_x = lax.axis_index("xline")
     my_z = lax.rem(me_i, N_Z)
     my_col = me_i // N_Z
     my_p = my_col * N_XL + me_x
+
+    def fetch(t):
+        return pltpu.make_async_copy(
+            traces_hbm.at[:, pl.ds(STARTS[t], WIDTHS[t])], traces.at[:, pl.ds(STARTS[t], WIDTHS[t])], in_sem.at[t]
+        )
+
+    def give(t):
+        lanes = pl.ds(STARTS[t], WIDTHS[t])
+        return pltpu.make_async_copy(out.at[:, :, :, lanes], out_hbm.at[:, :, :, lanes], out_sem.at[t])
+
+    for t in range(T):
+        fetch(t).start()
 
     def z_peer(k):
         z = lax.rem(my_z + k, N_Z)
@@ -150,7 +173,7 @@
     def row1_copy(t, k):
         z, peer = z_peer(k)
         return pltpu.make_async_remote_copy(
-            src_ref=send1.at[t, z], dst_ref=recv1.at[t, my_z],
+            src_ref=send1.at[t, z, :, wide_of(t)], dst_ref=recv1.at[t, my_z, :, wide_of(t)],
             send_sem=s1_send.at[t, k], recv_sem=s1_recv.at[t, k],
             device_id=peer, device_id_type=MESH,
         )
@@ -166,7 +189,7 @@
     def row2_copy(t, k):
         p, peer = p_peer(k)
         return pltpu.make_async_remote_copy(
-            src_ref=send2.at[t, p], dst_ref=recv2.at[t, my_p],
+            src_ref=send2.at[t, p, :, wide_of(t)], dst_ref=recv2.at[t, my_p, :, wide_of(t)],
             send_sem=s2_send.at[t, k], recv_sem=s2_recv.at[t, k],
             device_id=peer, device_id_type=MESH,
         )
@@ -176,16 +199,17 @@
         lab1_copy(k).start()
 
     def send_rows(t):
+        fetch(t).wait()
         picked = jnp.dot(
-            p1[...].reshape(N_Z * POOL, n), traces[:, t * w:(t + 1) * w], preferred_element_type=f32
-        )
-        send1[t] = picked.astype(bf16).reshape(N_Z, POOL, w)
+            p1[...].reshape(N_Z * POOL, n), traces[:, span(t)], preferred_element_type=f32
+        )
+        send1[t, :, :, wide_of(t)] = picked.astype(bf16).reshape(N_Z, POOL, WIDTHS[t])
 
         @pl.loop(1, N_Z)
         def _(k):
             row1_copy(t, k).start()
 
-        recv1[t, my_z] = send1[t, my_z]
+        recv1[t, my_z, :, wide_of(t)] = send1[t, my_z, :, wide_of(t)]
 
     send_rows(0)
     send_rows(1)
@@ -228,17 +252,18 @@
 
         if t + 2 < T:
             send_rows(t + 2)
-        arrived = recv1[t].reshape(N_Z * POOL, w)
+        arrived = recv1[t, :, :, wide_of(t)].reshape(N_Z * POOL, WIDTHS[t])
         half = ROWS // 2
         for g in range(2):
             moved = jnp.dot(p2[g * half:(g + 1) * half, :], arrived, preferred_element_type=f32)
-            send2[t, g * (N_P // 2):(g + 1) * (N_P // 2)] = moved.astype(bf16).reshape(N_P // 2, SLOTS, w)
+            moved = moved.astype(bf16).reshape(N_P // 2, SLOTS, WIDTHS[t])
+            send2[t, g * (N_P // 2):(g + 1) * (N_P // 2), :, wide_of(t)] = moved
 
         @pl.loop(1, N_P)
         def _(k):
             row2_copy(t, k).start()
 
-        recv2[t, my_p] = send2[t, my_p]
+        recv2[t, my_p, :, wide_of(t)] = send2[t, my_p, :, wide_of(t)]
 
     def selector():
         @pl.loop(1, N_P)
@@ -255,8 +280,8 @@
             lanes = pl.ds(pl.multiple_of(c * 128, 128), 128)
             sel[:, lanes] = onehot(iota((CELLS, 128), 0) == wide[0:1, lanes])
 
-        traces_per_cell = jnp.dot(sel[...], jnp.ones((ROWS, 128), bf16), preferred_element_type=f32)
-        count[...] = jnp.maximum(traces_per_cell, 1.0)
+        per_cell = jnp.dot(sel[...], jnp.ones((ROWS, 128), bf16), preferred_element_type=f32)
+        share[...] = 1.0 / jnp.maximum(per_cell, 1.0)
         flag_out[...] = jnp.broadcast_to(jnp.max(wide[1:2, :], axis=1, keepdims=True), (8, 128))
 
     def stack(t):
@@ -264,11 +289,11 @@
         def _(k):
             row2_copy(t, k).wait()
 
-        total = jnp.dot(sel[...], recv2[t].reshape(ROWS, w), preferred_element_type=f32)
-        parts = [total[:, c * 128:(c + 1) * 128] / count[...] for c in range(w // 128)]
+        total = jnp.dot(sel[...], recv2[t, :, :, wide_of(t)].reshape(ROWS, WIDTHS[t]), preferred_element_type=f32)
+        parts = [total[:, c * 128:(c + 1) * 128] * share[...] for c in range(WIDTHS[t] // 128)]
         top = jnp.abs(parts[0])
         for c, part in enumerate(parts):
-            lanes = slice(t * w + c * 128, t * w + (c + 1) * 128)
+            lanes = slice(STARTS[t] + c * 128, STARTS[t] + (c + 1) * 128)
             ext[BINS:2 * BINS, :, lanes] = part.reshape(BINS, OFFSETS, 128)
             top = jnp.maximum(top, jnp.abs(part))
         step = (jnp.max(top, axis=1, keepdims=True) * (1.01 / 32767.0)).astype(bf16)
@@ -279,36 +304,81 @@
             rim_q[t, :, c * 128:(c + 1) * 128] = jnp.round(part * fine).astype(i32).astype(jnp.int16)
         first_lane = onehot(iota((16, 128), 1) == 0)
         rim_s[t] = lax.dot_general(first_lane, step, NT, preferred_element_type=f32)[:8]
+        send_rim(t)
+
+    def size_copy(t, side):
+        return pltpu.make_async_remote_copy(
+            src_ref=rim_s.at[t], dst_ref=got_s.at[side, t],
+            send_sem=f_send.at[side, t], recv_sem=f_recv.at[side, t],
+            device_id=rim_peer(side), device_id_type=MESH,
+        )
+
+    def rim_copy(t, side, h):
+        return pltpu.make_async_remote_copy(
+            src_ref=rim_q.at[t, rim_half(h), wide_of(t)], dst_ref=got_q.at[side, t, rim_half(h), wide_of(t)],
+            send_sem=q_send.at[side, t, h], recv_sem=q_recv.at[side, t, h],
+            device_id=rim_peer(side), device_id_type=MESH,
+        )
+
+    def relay_copy(t, side):
+        return pltpu.make_async_remote_copy(
+            src_ref=rim_q.at[t, rim_half(1), wide_of(t)], dst_ref=relay.at[t, :, wide_of(t)],
+            send_sem=q_send.at[side, t, 1], recv_sem=r_recv.at[t],
+            device_id=(lax.rem(me_i + (N_Z if side == 0 else N_IL - N_Z), N_IL), me_x), device_id_type=MESH,
+        )
+
+    def onward_copy(t, side):
+        return pltpu.make_async_remote_copy(
+            src_ref=relay.at[t, :, wide_of(t)], dst_ref=got_q.at[side, t, rim_half(1), wide_of(t)],
+            send_sem=r_send.at[t], recv_sem=q_recv.at[side, t, 1],
+            device_id=(my_col * N_Z + (0 if side == 0 else N_Z - 1), me_x), device_id_type=MESH,
+        )
+
+    def rim_half(h):
+        return pl.ds(h * CELLS // 2, CELLS // 2)
+
+    def last_plane(side):
+        return my_z == (N_Z - 1 if side == 0 else 0)
+
+    def send_rim(t):
         for side in range(2):
-            for copy in rim_copies(t, side):
-                copy.start()
-
-    def rim_copies(t, side):
-        peer = rim_peer(side)
-        return (
-            pltpu.make_async_remote_copy(
-                src_ref=rim_s.at[t], dst_ref=got_s.at[side, t],
-                send_sem=f_send.at[side, t], recv_sem=f_recv.at[side, t],
-                device_id=peer, device_id_type=MESH,
-            ),
-            pltpu.make_async_remote_copy(
-                src_ref=rim_q.at[t], dst_ref=got_q.at[side, t],
-                send_sem=q_send.at[side, t], recv_sem=q_recv.at[side, t],
-                device_id=peer, device_id_type=MESH,
-            ),
-        )
+            size_copy(t, side).start()
+            rim_copy(t, side, 0).start()
+
+            @pl.when(last_plane(side))
+            def _():
+                relay_copy(t, side).start()
+
+            @pl.when(jnp.logical_not(last_plane(side)))
+            def _():
+                rim_copy(t, side, 1).start()
+
+    def pass_on(t):
+        for side in range(2):
+            @pl.when(last_plane(side))
+            def _():
+                relay_copy(t, side).wait_recv()
+                onward_copy(t, side).start()
+
+    def wait_rim(t, side):
+        size_copy(t, side).wait()
+        rim_copy(t, side, 0).wait()
+        rim_copy(t, side, 1).wait()
+
+        @pl.when(last_plane(side))
+        def _():
+            onward_copy(t, side).wait_send()
 
     def rim(t, side):
-        for copy in rim_copies(t, side):
-            copy.wait()
+        wait_rim(t, side)
         row = jnp.broadcast_to(got_s[side, t][0:1, :], (128, CELLS)).astype(bf16)
         size = lax.dot_general(eye[...], row, NT, preferred_element_type=f32)
         outside = me_i == (0 if side == 0 else N_IL - 1)
         size = size * jnp.where(outside, 0.0, 1.0)
         base = 0 if side == 0 else 2 * BINS
-        for c in range(w // 128):
+        for c in range(WIDTHS[t] // 128):
             value = got_q[side, t, :, c * 128:(c + 1) * 128].astype(f32)
-            lanes = slice(t * w + c * 128, t * w + (c + 1) * 128)
+            lanes = slice(STARTS[t] + c * 128, STARTS[t] + (c + 1) * 128)
             ext[base:base + BINS, :, lanes] = (value * size).reshape(BINS, OFFSETS, 128)
 
     n_il, n_xl = dips.shape
@@ -316,64 +386,68 @@
     def edge_copy(t, side):
         x = lax.rem(me_x + (1 if side == 0 else N_XL - 1), N_XL)
         return pltpu.make_async_remote_copy(
-            src_ref=edge.at[side, t], dst_ref=got_e.at[side, t],
+            src_ref=edge.at[side, t, :, :, :, wide_of(t)], dst_ref=got_e.at[side, t, :, :, :, wide_of(t)],
             send_sem=e_send.at[side, t], recv_sem=e_recv.at[side, t],
             device_id=(me_i, x), device_id_type=MESH,
         )
 
     def inline_pass(t):
-        ks = range(t * w // 128, (t + 1) * w // 128)
+        ks = range(STARTS[t] // 128, (STARTS[t] + WIDTHS[t]) // 128)
 
         def column(x):
             for i in range(n_il):
-                acc = steer(lambda j, i=i: (ext, ((i + 4 + j) * n_xl + x,)), dips[i, x], samples // 128, ks)
+                acc = steer(lambda j, i=i: (ext, ((i + 4 + j) * n_xl + x,)), dips[i, x], parts, ks)
                 for k, part in zip(ks, acc):
                     out[i, x + 4, :, k * 128:(k + 1) * 128] = part
 
-        pl.loop(0, 4)(column)
-        pl.loop(n_xl - 4, n_xl)(column)
-        lanes = slice(t * w, (t + 1) * w)
-        edge[0, t] = out[:, n_xl:n_xl + 4, :, lanes]
-        edge[1, t] = out[:, 4:8, :, lanes]
+        pl.loop(0, 4, unroll=UNROLL)(column)
+        pl.loop(n_xl - 4, n_xl, unroll=UNROLL)(column)
+        edge[0, t, :, :, :, wide_of(t)] = out[:, n_xl:n_xl + 4, :, span(t)]
+        edge[1, t, :, :, :, wide_of(t)] = out[:, 4:8, :, span(t)]
         for side in range(2):
             edge_copy(t, side).start()
-        pl.loop(4, n_xl - 4)(column)
+        pl.loop(4, n_xl - 4, unroll=UNROLL)(column)
 
     def edges(t):
-        lanes = slice(t * w, (t + 1) * w)
+        lanes = span(t)
         for side in range(2):
             edge_copy(t, side).wait()
             outside = me_x == (0 if side == 0 else N_XL - 1)
-            value = got_e[side, t] * jnp.where(outside, 0.0, 1.0)
+            value = got_e[side, t, :, :, :, wide_of(t)] * jnp.where(outside, 0.0, 1.0)
             if side == 0:
                 out[:, 0:4, :, lanes] = value
             else:
                 out[:, n_xl + 4:, :, lanes] = value
+        give(t).start()
 
     def rims(t):
         for side in range(2):
             rim(t, side)
 
-    for t in range(T + 3):
+    for t in range(T + 5):
         if t < T:
             forward(t)
         if t == 0:
             selector()
+        if 0 <= t - 2 < T:
+            pass_on(t - 2)
         if 0 <= t - 1 < T:
             stack(t - 1)
-        if 0 <= t - 2 < T:
-            rims(t - 2)
-        if 0 <= t - 3 < T - 1:
-            inline_pass(t - 3)
-    inline_pass(T - 1)
+        if 0 <= t - 3 < T:
+            rims(t - 3)
+        if 0 <= t - 4 < T:
+            inline_pass(t - 4)
+        if 0 <= t - 5 < T:
+            edges(t - 5)
     for t in range(T):
-        edges(t)
+        give(t).wait()
 
 
 def route(dips, traces, dest, bins, offs):
     n, samples = traces.shape
     n_il, n_xl = dips.shape
-    w = samples // T
+    w = W
+    hbm = pl.BlockSpec(memory_space=pltpu.HBM)
     vmem = pl.BlockSpec(memory_space=pltpu.VMEM)
     dma = pltpu.SemaphoreType.DMA
     return pl.pallas_call(
@@ -382,9 +456,11 @@
             jax.ShapeDtypeStruct((n_il, n_xl + 8, OFFSETS, samples), f32),
             jax.ShapeDtypeStruct((8, 128), i32),
         ),
-        in_specs=[pl.BlockSpec(memory_space=pltpu.SMEM)] + [vmem] * 4,
-        out_specs=(vmem, vmem),
+        in_specs=[pl.BlockSpec(memory_space=pltpu.SMEM), hbm] + [vmem] * 3,
+        out_specs=(hbm, vmem),
         scratch_shapes=[
+            pltpu.VMEM((n, samples), bf16),
+            pltpu.VMEM((n_il, n_xl + 8, OFFSETS, samples), f32),
             pltpu.VMEM((3 * BINS, OFFSETS, samples), f32),
             pltpu.VMEM((8, n), f32),
             pltpu.VMEM((n, n), bf16),
@@ -406,11 +482,13 @@
             pltpu.VMEM((T, 8, CELLS), f32),
             pltpu.VMEM((2, T, CELLS, w), jnp.int16),
             pltpu.VMEM((2, T, 8, CELLS), f32),
+            pltpu.VMEM((T, CELLS // 2, w), jnp.int16),
             pltpu.VMEM((2, T, n_il, 4, OFFSETS, w), f32),
             pltpu.VMEM((2, T, n_il, 4, OFFSETS, w), f32),
             dma((T, N_Z)), dma((T, N_Z)), dma((N_Z,)), dma((N_Z,)),
             dma((T, N_P)), dma((T, N_P)), dma((N_P,)), dma((N_P,)),
-            dma((2, T)), dma((2, T)), dma((2, T)), dma((2, T)), dma((2, T)), dma((2, T)),
+            dma((2, T, 2)), dma((2, T, 2)), dma((2, T)), dma((2, T)), dma((2, T)), dma((2, T)),
+            dma((T,)), dma((T,)), dma((T,)), dma((T,)),
         ],
         compiler_params=pltpu.CompilerParams(
             collective_id=0, has_side_effects=True, vmem_limit_bytes=48 * 1024 * 1024
@@ -421,10 +499,11 @@
 def xline_kernel(dips, ext, out, turned):
     n_xl, samples = out.shape[2], out.shape[3]
     il = pl.program_id(0)
+    first = pl.program_id(1) * n_xl
     ks = range(samples // 128)
 
     def column(x, carry):
-        acc = steer(lambda j: (ext, (0, x + 4 + j)), dips[il, x], len(ks), ks)
+        acc = steer(lambda j: (ext, (0, first + x + 4 + j)), dips[il, first + x], len(ks), ks)
         for k, part in zip(ks, acc):
             turned[k, pl.ds(x, OFFSETS, stride=n_xl), :] = part
         return carry
@@ -437,16 +516,17 @@
 def xline_pass(dips, ext):
     n_il, n_xl = dips.shape
     samples = ext.shape[-1]
+    step = n_xl
     return pl.pallas_call(
         xline_kernel,
-        grid=(n_il,),
+        grid=(n_il, n_xl // step),
         out_shape=jax.ShapeDtypeStruct((OFFSETS, n_il, n_xl, samples), f32),
         in_specs=[
             pl.BlockSpec(memory_space=pltpu.SMEM),
-            pl.BlockSpec((1, n_xl + 8, OFFSETS, samples), lambda s: (s, 0, 0, 0)),
+            pl.BlockSpec((1, n_xl + 8, OFFSETS, samples), lambda s, h: (s, 0, 0, 0)),
         ],
-        out_specs=pl.BlockSpec((OFFSETS, 1, n_xl, samples), lambda s: (0, s, 0, 0)),
-        scratch_shapes=[pltpu.VMEM((samples // 128, OFFSETS * n_xl, 128), f32)],
+        out_specs=pl.BlockSpec((OFFSETS, 1, step, samples), lambda s, h: (0, s, h, 0)),
+        scratch_shapes=[pltpu.VMEM((samples // 128, OFFSETS * step, 128), f32)],
         compiler_params=pltpu.CompilerParams(vmem_limit_bytes=60 * 1024 * 1024),
     )(dips, ext)
 

time: 114 us -> 103 us (0.904)
  the two profiles are of different devices: /device:TPU:2 before, /device:TPU:64 now
where the time goes in v4:
time: 103 us
  Pallas kernels  101 us (98%)
    pallas_call x1, Pallas kernels, route(): pl.pallas_call(route_kernel, out_shape=(jax.ShapeDtypeStruct((n_il, n_xl...  94.3 us
    pallas_call x1, Pallas kernels, xline_pass(): pl.pallas_call(xline_kernel, grid=(n_il, n_xl // step), out_shape=jax.Sha...  7.18 us

profile of v4, /device:TPU:64, one launch (start us, length us, event | category | flops | bytes accessed | tf_op | source)
XLA Modules:
  0.0 102.6 jit_solution(8378316128834548771)
XLA Ops:
  0.0 94.3 %shard_map.66 = (f32[4,24,8,1024]{3,2,1,0:T(8,128)S(1)}, s32[8,128]{1,0:T(8,128)S(1)}) custom-call(s32[4,16]{1,0:T(4,128)} %dips.1, bf16[512,1024]{1,0:T(8,128)(2,1)} %traces_hbm.1, s32[1,512]{1,0:T(1,128)} %bitcast.33, s32[1,512]{1,0:T(1,128)} %bitcast.37, s32[1,512]{1,0:T(1,128)} %bitcast.38), custom_call_target="tpu_custom_call" | custom-call | tf_op jit(solution)/shard_map/pallas_call | solution.py:453
  94.3 0.5 slice.525
  95.4 7.2 %conditional.1 = (f32[8,4,16,1024]{3,2,1,0:T(8,128)}) conditional(s32[]{:T(128)} %bitcast.11, (s32[4,16]{1,0:T(4,128)}, f32[4,24,8,1024]{3,2,1,0:T(8,128)S(1)}) %tuple.11, (s32[4,16]{1,0:T(4,128)}, s32[4,16]{1,0:T(4,128)}, s32[512,1]{0,1:T(1,128)}, s32[512]{0:T(512)}, s32[512]{0:T(512)}, /*index=5*/bf16[512,1024]{1,0:T(8,128)(2,1)}) %tuple.12), branch_computations={%region_0.0_spmd, %region_1.8_spmd} | conditional | flops 1742528768 | bytes 319490240 | solution.py:617
  95.4 7.2 %branch_0_fun.1 = f32[8,4,16,1024]{3,2,1,0:T(8,128)} custom-call(s32[4,16]{1,0:T(4,128)} %get-tuple-element.24.dips, f32[4,24,8,1024]{3,2,1,0:T(8,128)S(1)} %get-tuple-element.25.ext), custom_call_target="tpu_custom_call" | custom-call | tf_op jit(solution)/shard_map/cond/branch_0_fun/pallas_call | solution.py:520

commit v5 on v4

--- a/solution.py
+++ b/solution.py
@@ -166,7 +166,7 @@
         z, peer = z_peer(k)
         return pltpu.make_async_remote_copy(
             src_ref=lab1s.at[z], dst_ref=lab1r.at[my_z],
-            send_sem=l1_send.at[k], recv_sem=l1_recv.at[k],
+            send_sem=l1_send.at[0], recv_sem=l1_recv.at[0],
             device_id=peer, device_id_type=MESH,
         )
 
@@ -174,7 +174,7 @@
         z, peer = z_peer(k)
         return pltpu.make_async_remote_copy(
             src_ref=send1.at[t, z, :, wide_of(t)], dst_ref=recv1.at[t, my_z, :, wide_of(t)],
-            send_sem=s1_send.at[t, k], recv_sem=s1_recv.at[t, k],
+            send_sem=s1_send.at[t], recv_sem=s1_recv.at[t],
             device_id=peer, device_id_type=MESH,
         )
 
@@ -182,7 +182,7 @@
         p, peer = p_peer(k)
         return pltpu.make_async_remote_copy(
             src_ref=lab2s.at[p], dst_ref=lab2r.at[my_p],
-            send_sem=l2_send.at[k], recv_sem=l2_recv.at[k],
+            send_sem=l2_send.at[0], recv_sem=l2_recv.at[0],
             device_id=peer, device_id_type=MESH,
         )
 
@@ -190,8 +190,29 @@
         p, peer = p_peer(k)
         return pltpu.make_async_remote_copy(
             src_ref=send2.at[t, p, :, wide_of(t)], dst_ref=recv2.at[t, my_p, :, wide_of(t)],
-            send_sem=s2_send.at[t, k], recv_sem=s2_recv.at[t, k],
+            send_sem=s2_send.at[t], recv_sem=s2_recv.at[t],
             device_id=peer, device_id_type=MESH,
+        )
+
+    def all_of(src, dst, send, recv, peer):
+        return pltpu.make_async_remote_copy(
+            src_ref=src, dst_ref=dst, send_sem=send, recv_sem=recv, device_id=peer, device_id_type=MESH
+        )
+
+    z_others, p_others = pl.ds(0, N_Z - 1), pl.ds(0, N_P - 1)
+    lab1_all = all_of(lab1s.at[z_others], lab1r.at[z_others], l1_send.at[0], l1_recv.at[0], z_peer(1)[1])
+    lab2_all = all_of(lab2s.at[p_others], lab2r.at[p_others], l2_send.at[0], l2_recv.at[0], p_peer(1)[1])
+
+    def row1_all(t):
+        return all_of(
+            send1.at[t, z_others, :, wide_of(t)], recv1.at[t, z_others, :, wide_of(t)],
+            s1_send.at[t], s1_recv.at[t], z_peer(1)[1],
+        )
+
+    def row2_all(t):
+        return all_of(
+            send2.at[t, p_others, :, wide_of(t)], recv2.at[t, p_others, :, wide_of(t)],
+            s2_send.at[t], s2_recv.at[t], p_peer(1)[1],
         )
 
     @pl.loop(1, N_Z)
@@ -214,9 +235,7 @@
     send_rows(0)
     send_rows(1)
 
-    @pl.loop(1, N_Z)
-    def _(k):
-        lab1_copy(k).wait()
+    lab1_all.wait_recv()
 
     lab = jnp.concatenate([lab1r[z][:, :POOL] for z in range(N_Z)], axis=1)
     code = lab[1:2, :]
@@ -246,9 +265,7 @@
         lab2_copy(k).start()
 
     def forward(t):
-        @pl.loop(1, N_Z)
-        def _(k):
-            row1_copy(t, k).wait()
+        row1_all(t).wait_recv()
 
         if t + 2 < T:
             send_rows(t + 2)
@@ -266,9 +283,8 @@
         recv2[t, my_p, :, wide_of(t)] = send2[t, my_p, :, wide_of(t)]
 
     def selector():
-        @pl.loop(1, N_P)
-        def _(k):
-            lab2_copy(k).wait()
+        lab2_all.wait_recv()
+        lab1_all.wait_send()
 
         @pl.loop(0, N_P // 8)
         def _(g):
@@ -285,9 +301,7 @@
         flag_out[...] = jnp.broadcast_to(jnp.max(wide[1:2, :], axis=1, keepdims=True), (8, 128))
 
     def stack(t):
-        @pl.loop(1, N_P)
-        def _(k):
-            row2_copy(t, k).wait()
+        row2_all(t).wait_recv()
 
         total = jnp.dot(sel[...], recv2[t, :, :, wide_of(t)].reshape(ROWS, WIDTHS[t]), preferred_element_type=f32)
         parts = [total[:, c * 128:(c + 1) * 128] * share[...] for c in range(WIDTHS[t] // 128)]
@@ -361,13 +375,21 @@
                 onward_copy(t, side).start()
 
     def wait_rim(t, side):
-        size_copy(t, side).wait()
-        rim_copy(t, side, 0).wait()
-        rim_copy(t, side, 1).wait()
-
-        @pl.when(last_plane(side))
-        def _():
-            onward_copy(t, side).wait_send()
+        size_copy(t, side).wait_recv()
+        rim_copy(t, side, 0).wait_recv()
+        rim_copy(t, side, 1).wait_recv()
+
+    def sent(t):
+        row1_all(t).wait_send()
+        row2_all(t).wait_send()
+        for side in range(2):
+            size_copy(t, side).wait_send()
+            rim_copy(t, side, 0).wait_send()
+            rim_copy(t, side, 1).wait_send()
+
+            @pl.when(last_plane(side))
+            def _():
+                onward_copy(t, side).wait_send()
 
     def rim(t, side):
         wait_rim(t, side)
@@ -419,6 +441,7 @@
             else:
                 out[:, n_xl + 4:, :, lanes] = value
         give(t).start()
+        sent(t)
 
     def rims(t):
         for side in range(2):
@@ -439,6 +462,7 @@
             inline_pass(t - 4)
         if 0 <= t - 5 < T:
             edges(t - 5)
+    lab2_all.wait_send()
     for t in range(T):
         give(t).wait()
 
@@ -485,8 +509,8 @@
             pltpu.VMEM((T, CELLS // 2, w), jnp.int16),
             pltpu.VMEM((2, T, n_il, 4, OFFSETS, w), f32),
             pltpu.VMEM((2, T, n_il, 4, OFFSETS, w), f32),
-            dma((T, N_Z)), dma((T, N_Z)), dma((N_Z,)), dma((N_Z,)),
-            dma((T, N_P)), dma((T, N_P)), dma((N_P,)), dma((N_P,)),
+            dma((T,)), dma((T,)), dma((1,)), dma((1,)),
+            dma((T,)), dma((T,)), dma((1,)), dma((1,)),
             dma((2, T, 2)), dma((2, T, 2)), dma((2, T)), dma((2, T)), dma((2, T)), dma((2, T)),
             dma((T,)), dma((T,)), dma((T,)), dma((T,)),
         ],

time: 103 us -> 97.3 us (0.945)
  Pallas kernels: 101 us -> 96 us
    pallas_call x1, Pallas kernels: 94.3 us -> 88.8 us  [route(): pl.pallas_call(route_kernel, out_shape=(jax.ShapeDtypeStruct((n_il, n_xl...]
where the time goes in v5:
time: 97.3 us; the launch traced here: 97.2 us
  Pallas kernels  96 us (99%)
    pallas_call x1, Pallas kernels, route(): pl.pallas_call(route_kernel, out_shape=(jax.ShapeDtypeStruct((n_il, n_xl...  88.8 us
    pallas_call x1, Pallas kernels, xline_pass(): pl.pallas_call(xline_kernel, grid=(n_il, n_xl // step), out_shape=jax.Sha...  7.18 us

profile of v5, /device:TPU:64, one launch (start us, length us, event | category | flops | bytes accessed | tf_op | source)
XLA Modules:
  0.0 97.2 jit_solution(2696049260576245603)
XLA Ops:
  0.0 88.8 %shard_map.66 = (f32[4,24,8,1024]{3,2,1,0:T(8,128)S(1)}, s32[8,128]{1,0:T(8,128)S(1)}) custom-call(s32[4,16]{1,0:T(4,128)} %dips.1, bf16[512,1024]{1,0:T(8,128)(2,1)} %traces_hbm.1, s32[1,512]{1,0:T(1,128)} %bitcast.33, s32[1,512]{1,0:T(1,128)} %bitcast.37, s32[1,512]{1,0:T(1,128)} %bitcast.38), custom_call_target="tpu_custom_call" | custom-call | tf_op jit(solution)/shard_map/pallas_call | solution.py:477
  88.9 0.5 slice.525
  90.0 7.2 %conditional.1 = (f32[8,4,16,1024]{3,2,1,0:T(8,128)}) conditional(s32[]{:T(128)} %bitcast.11, (s32[4,16]{1,0:T(4,128)}, f32[4,24,8,1024]{3,2,1,0:T(8,128)S(1)}) %tuple.11, (s32[4,16]{1,0:T(4,128)}, s32[4,16]{1,0:T(4,128)}, s32[512,1]{0,1:T(1,128)}, s32[512]{0:T(512)}, s32[512]{0:T(512)}, /*index=5*/bf16[512,1024]{1,0:T(8,128)(2,1)}) %tuple.12), branch_computations={%region_0.0_spmd, %region_1.8_spmd} | conditional | flops 1742528768 | bytes 319490240 | solution.py:641
  90.0 7.2 %branch_0_fun.1 = f32[8,4,16,1024]{3,2,1,0:T(8,128)} custom-call(s32[4,16]{1,0:T(4,128)} %get-tuple-element.24.dips, f32[4,24,8,1024]{3,2,1,0:T(8,128)S(1)} %get-tuple-element.25.ext), custom_call_target="tpu_custom_call" | custom-call | tf_op jit(solution)/shard_map/cond/branch_0_fun/pallas_call | solution.py:544

commit v6 on v5

--- a/solution.py
+++ b/solution.py
@@ -119,7 +119,7 @@
     def _(k):
         pl.semaphore_signal(barrier, inc=1, device_id=z_peer(k)[1], device_id_type=MESH)
 
-    @pl.loop(1, N_P)
+    @pl.loop(1, N_P, unroll=4)
     def _(k):
         pl.semaphore_signal(barrier, inc=1, device_id=p_peer(k)[1], device_id_type=MESH)
 
@@ -226,7 +226,7 @@
         )
         send1[t, :, :, wide_of(t)] = picked.astype(bf16).reshape(N_Z, POOL, WIDTHS[t])
 
-        @pl.loop(1, N_Z)
+        @pl.loop(1, N_Z, unroll=7)
         def _(k):
             row1_copy(t, k).start()
 
@@ -276,7 +276,7 @@
             moved = moved.astype(bf16).reshape(N_P // 2, SLOTS, WIDTHS[t])
             send2[t, g * (N_P // 2):(g + 1) * (N_P // 2), :, wide_of(t)] = moved
 
-        @pl.loop(1, N_P)
+        @pl.loop(1, N_P, unroll=4)
         def _(k):
             row2_copy(t, k).start()
 
@@ -532,7 +532,7 @@
             turned[k, pl.ds(x, OFFSETS, stride=n_xl), :] = part
         return carry
 
-    lax.fori_loop(0, n_xl, column, 0, unroll=8)
+    lax.fori_loop(0, n_xl, column, 0, unroll=16)
     for k in ks:
         out[:, 0, :, k * 128:(k + 1) * 128] = turned[k].reshape(OFFSETS, n_xl, 128)
 

time: 97.3 us -> 98.3 us (1.010)
  Pallas kernels: 96 us -> 97 us
    pallas_call x1, Pallas kernels: 88.8 us -> 90.2 us  [route(): pl.pallas_call(route_kernel, out_shape=(jax.ShapeDtypeStruct((n_il, n_xl...]
where the time goes in v6:
time: 98.3 us; the launch traced here: 98.2 us
  Pallas kernels  97 us (99%)
    pallas_call x1, Pallas kernels, route(): pl.pallas_call(route_kernel, out_shape=(jax.ShapeDtypeStruct((n_il, n_xl...  90.2 us
    pallas_call x1, Pallas kernels, xline_pass(): pl.pallas_call(xline_kernel, grid=(n_il, n_xl // step), out_shape=jax.Sha...  6.76 us

profile of v6, /device:TPU:64, one launch (start us, length us, event | category | flops | bytes accessed | tf_op | source)
XLA Modules:
  0.0 98.2 jit_solution(14022303830871753977)
XLA Ops:
  0.0 90.2 %shard_map.66 = (f32[4,24,8,1024]{3,2,1,0:T(8,128)S(1)}, s32[8,128]{1,0:T(8,128)S(1)}) custom-call(s32[4,16]{1,0:T(4,128)} %dips.1, bf16[512,1024]{1,0:T(8,128)(2,1)} %traces_hbm.1, s32[1,512]{1,0:T(1,128)} %bitcast.33, s32[1,512]{1,0:T(1,128)} %bitcast.37, s32[1,512]{1,0:T(1,128)} %bitcast.38), custom_call_target="tpu_custom_call" | custom-call | tf_op jit(solution)/shard_map/pallas_call | solution.py:477
  90.2 0.5 slice.525
  91.4 6.8 %conditional.1 = (f32[8,4,16,1024]{3,2,1,0:T(8,128)}) conditional(s32[]{:T(128)} %bitcast.11, (s32[4,16]{1,0:T(4,128)}, f32[4,24,8,1024]{3,2,1,0:T(8,128)S(1)}) %tuple.11, (s32[4,16]{1,0:T(4,128)}, s32[4,16]{1,0:T(4,128)}, s32[512,1]{0,1:T(1,128)}, s32[512]{0:T(512)}, s32[512]{0:T(512)}, /*index=5*/bf16[512,1024]{1,0:T(8,128)(2,1)}) %tuple.12), branch_computations={%region_0.0_spmd, %region_1.8_spmd} | conditional | flops 1742528768 | bytes 319490240 | solution.py:641
  91.4 6.8 %branch_0_fun.1 = f32[8,4,16,1024]{3,2,1,0:T(8,128)} custom-call(s32[4,16]{1,0:T(4,128)} %get-tuple-element.24.dips, f32[4,24,8,1024]{3,2,1,0:T(8,128)S(1)} %get-tuple-element.25.ext), custom_call_target="tpu_custom_call" | custom-call | tf_op jit(solution)/shard_map/cond/branch_0_fun/pallas_call | solution.py:544
